TPU v7x, 1024 devices: a whole 4x4x32 slice. The times are simulated.
1024 devices in a mesh: doc: 64 (over y_hi, z), label: 16 (over x, y_lo, core).
Axes of the slice: x: 4, y: 4 (y_hi: 2, y_lo: 2; y = y_hi * 2 + y_lo), z: 32, core: 2. Of those that a mesh axis runs over, the one named last changes fastest.
Arguments:
- doc_emb: bfloat16 [65536, 768], P(('doc', 'label'))
- label_emb: bfloat16 [16384, 768], P(('label', 'doc'))
- short_blocks: int32 [256, 32], replicated, may hold values from 0 to 127, as said below
- short_len: int32 [256], replicated, may hold values from 1 to 32, as said below
- positives: int32 [65536, 8], P('doc'), may hold values from 0 to 16383, as said below
Outputs:
- doc_grad: float32 [65536, 768], P(('doc', 'label'))
Inputs may be any that keep to these rules, and one draw needn't show every extreme that they name: `short_blocks`: each row lists, in a random order, 2 distinct blocks out of every run of 8 consecutive label blocks k * 8 to (k + 1) * 8 - 1. `short_len`: some row is full. `positives`: every positive of a document lies in a label block among the live entries of its block's list; ids may repeat.
All inputs are finite; a program needn't handle non-finite values.
Results may differ from a plain program's by a relative error of at most 0.0045.
Values may be sent and summed in bfloat16 or wider, within the bound.
No kernel may reach another device: no remote copies, remote signals or barrier semaphores. Data moves between devices by JAX's collectives and lax.ppermute only.
A program may use at most 32 MiB of HBM per device.

v0:
```python
import jax
import jax.numpy as jnp
from jax import lax
from jax.sharding import PartitionSpec as P

DOC_BLK = 256
LAB_BLK = 128
POS = 8


SCALE = 16.0


def unit_rows(matrix):
    widened = matrix.astype(jnp.float32)
    row_norm = jnp.sqrt(jnp.sum(widened * widened, axis=-1, keepdims=True) + 1e-06)
    return (widened / row_norm, row_norm)


def body(doc_emb, label_emb, short_blocks, short_len, positives):
    group_docs = lax.all_gather(doc_emb, "label", axis=0, tiled=True)
    doc_unit_all, _ = unit_rows(group_docs)
    doc_half = doc_unit_all.astype(jnp.bfloat16)
    row_count = group_docs.shape[0]
    feat_width = group_docs.shape[1]
    block_count = row_count // DOC_BLK
    doc_index = lax.axis_index("doc")
    label_shard = lax.axis_index("label")
    shard_rows = label_emb.shape[0] * lax.axis_size("doc")
    shard_first = label_shard * shard_rows
    listed = lax.dynamic_slice_in_dim(short_blocks, doc_index * block_count, block_count, 0)
    list_len = lax.dynamic_slice_in_dim(short_len, doc_index * block_count, block_count, 0)
    live_slots = jnp.arange(listed.shape[1], dtype=jnp.int32)[None, :] < list_len[:, None]
    panels = lax.all_gather(label_emb, "doc", axis=0, tiled=True)
    panel_unit, _ = unit_rows(panels)
    panel_half = panel_unit.astype(jnp.bfloat16)
    local_blocks = shard_rows // LAB_BLK
    local_ids = listed - label_shard * local_blocks
    block_grid = jnp.arange(local_blocks, dtype=jnp.int32)
    active = jnp.any(
        (local_ids[:, :, None] == block_grid[None, None, :]) & live_slots[:, :, None], axis=1
    )
    active = active.astype(jnp.float32)
    labels = shard_first + jnp.arange(shard_rows, dtype=jnp.int32)
    scores = SCALE * lax.dot_general(
        doc_half, panel_half, (((1,), (1,)), ((), ())), preferred_element_type=jnp.float32
    )
    hit_count = jnp.zeros(scores.shape, jnp.float32)
    for column in range(POS):
        hit_count = hit_count + (positives[:, column][:, None] == labels[None, :]).astype(
            jnp.float32
        )
    target = jnp.minimum(hit_count, 1.0)
    pair_coef = (SCALE * (jax.nn.sigmoid(scores) - target)).reshape(
        block_count, DOC_BLK, local_blocks, LAB_BLK
    )
    pair_coef = (
        (pair_coef * active[:, None, :, None]).reshape(row_count, shard_rows).astype(jnp.bfloat16)
    )
    doc_grads = jnp.dot(pair_coef, panel_half, preferred_element_type=jnp.float32)
    pieces = lax.all_to_all(doc_grads, "label", split_axis=0, concat_axis=0, tiled=True)
    summed = jnp.sum(pieces.reshape(lax.axis_size("label"), -1, feat_width), axis=0)
    own_unit, own_norm = unit_rows(doc_emb)
    radial = jnp.sum(summed * own_unit, axis=-1, keepdims=True)
    return (summed - radial * own_unit) / own_norm


def solution(mesh):
    placed = (P(("doc", "label"), None), P(("label", "doc"), None), P(), P(), P("doc", None))
    return jax.shard_map(
        body, mesh=mesh, in_specs=placed, out_specs=P(("doc", "label"), None), check_vma=False
    )
```

profile of v0, /device:TPU:1, one launch (start us, length us, event | category | flops | bytes accessed | tf_op | source)
XLA Modules:
  0.0 411.4 jit_solution(1107100673791511202)
XLA Ops:
  6.5 0.0 copy-start
  6.5 0.0 all-gather.3.cloned.1.call-start
  6.5 0.7 all-gather.3.cloned.1.call-update
  7.3 0.0 all-gather.5.cloned.1.call-start
  7.3 0.7 all-gather.5.cloned.1.call-update
  8.0 0.0 copy-done
  8.0 0.1 constant_dynamic-slice_fusion
  8.1 0.1 copy.9
  8.2 0.8 dynamic_slice.7
  8.9 0.1 iota_compare_fusion.1
  9.0 0.1 fusion.11
  9.2 1.1 fusion.14
  10.3 59.7 %all-gather.3.cloned.1.call-done = bf16[1024,768]{1,0:T(8,128)(2,1)} async-done(((bf16[64,768]{1,0:T(8,128)(2,1)}), bf16[1024,768]{1,0:T(8,128)(2,1)}) %all-gather.3.cloned.1.call-update) | async-done | bytes 1572880 | tf_op jit(solution)/shard_map/all_gather | solution.py:21
  70.0 0.0 copy-start.2
  70.0 1.9 fusion.1
  71.9 256.0 %all-gather.5.cloned.1.call-done = bf16[1024,768]{1,0:T(8,128)(2,1)} async-done(((bf16[16,768]{1,0:T(8,128)(2,1)}), bf16[1024,768]{1,0:T(8,128)(2,1)}) %all-gather.5.cloned.1.call-update) | async-done | bytes 1572880 | tf_op jit(solution)/shard_map/all_gather | solution.py:34
  327.9 0.0 copy-start.1
  327.9 1.9 fusion.3
  329.8 0.3 mul.54
  330.1 0.0 copy-done.2
  330.2 0.0 copy-done.1
  330.2 5.4 %fusion = bf16[1024,1024]{1,0:T(8,128)(2,1)S(1)} fusion(f32[128,8,8,128]{3,2,1,0:T(8,128)S(1)} %bitcast.19, s32[1024]{0:T(1024)S(1)} %iota_add_fusion, s32[1024]{0:T(1024)S(1)} %bitcast.26, s32[1024]{0:T(1024)S(1)} %bitcast.27, s32[1024]{0:T(1024)S(1)} %bitcast.21, s32[1024]{0:T(1024)S(1)} %bitcast.22, s32[1024]{0:T(1024)S(1)} %bitcast.23, ...), kind=kOutput, calls=%fused_computation.1 | convolution fusion | flops 1648885760 | bytes 9482240 | tf_op jit(solution)/shard_map/dot_general | solution.py:45
  335.6 3.6 fusion.6
  339.2 0.0 copy-start.3
  339.2 24.8 %all-to-all-start = ((f32[16,64,768]{2,1,0:T(8,128)}), f32[16,64,768]{2,1,0:T(8,128)S(1)}, u32[]{:S(2)}, u32[]{:S(2)}) async-start(f32[16,64,768]{2,1,0:T(8,128)} %fusion.6), calls=%async_computation | async-start | bytes 6291456 | tf_op jit(solution)/shard_map/all_to_all | solution.py:61
  363.9 0.0 copy-done.3
  363.9 0.1 fusion.9
  364.1 39.3 %all-to-all-done = f32[16,64,768]{2,1,0:T(8,128)S(1)} async-done(((f32[16,64,768]{2,1,0:T(8,128)}), f32[16,64,768]{2,1,0:T(8,128)S(1)}, u32[]{:S(2)}, u32[]{:S(2)}) %all-to-all-start) | async-done | bytes 3145760 | tf_op jit(solution)/shard_map/all_to_all | solution.py:61
  403.4 0.2 reduce_sum.47
  403.6 0.2 multiply_reduce_fusion
  403.8 0.8 subtract_divide_fusion
  (6 shorter events, 0.0 us)
Async XLA Ops:
  6.5 1.5 copy-start
  6.5 63.4 %all-gather.3.cloned.1.call-start = ((), (), s32[]{:S(2)}) async-start(), calls=%async_computation.1 | async-start | bytes 1671168 | tf_op jit(solution)/shard_map/all_gather | solution.py:21
  7.3 320.6 %all-gather.5.cloned.1.call-start = ((), (), s32[]{:S(2)}) async-start(), calls=%async_computation.2 | async-start | bytes 1597440 | tf_op jit(solution)/shard_map/all_gather | solution.py:34
  70.0 260.2 %copy-start.2 = (bf16[1024,768]{1,0:T(8,128)(2,1)S(1)}, bf16[1024,768]{1,0:T(8,128)(2,1)}, u32[]{:S(2)}) copy-start(bf16[1024,768]{1,0:T(8,128)(2,1)} %all-gather.3.cloned.1.call-done) | copy-start | bytes 4718596
  327.9 2.3 copy-start.1
  339.2 24.8 %copy-start.3 = (bf16[64,768]{1,0:T(8,128)(2,1)S(1)}, bf16[64,768]{1,0:T(8,128)(2,1)}, u32[]{:S(2)}) copy-start(bf16[64,768]{1,0:T(8,128)(2,1)} %param.5) | copy-start | bytes 294916
  339.2 64.2 %all-to-all-start = ((f32[16,64,768]{2,1,0:T(8,128)}), f32[16,64,768]{2,1,0:T(8,128)S(1)}, u32[]{:S(2)}, u32[]{:S(2)}) async-start(f32[16,64,768]{2,1,0:T(8,128)} %fusion.6), calls=%async_computation | async-start | bytes 6291456 | tf_op jit(solution)/shard_map/all_to_all | solution.py:61
Sparse Core Ops, SparseCore 0:
  10.1 59.8 all-gather.2
  74.2 253.6 all-gather.4
where the time goes:
time: 414 us; the launch traced here: 411 us
  waiting for transfers between devices  356 us (86%)
  starting transfers between devices  24.8 us (6%)
  between operations  13.5 us (3%)
  matrix products  9 us (2%)
  other arithmetic  5.32 us (1%)
    all_gather x1, waiting for transfers between devices, body(): panels = lax.all_gather(label_emb, 'doc', axis=0, tiled=True)  256 us
    all_gather x1, waiting for transfers between devices, body(): group_docs = lax.all_gather(doc_emb, 'label', axis=0, tiled=True)  59.7 us
    all_to_all x1, waiting for transfers between devices, body(): lax.all_to_all(doc_grads, 'label', split_axis=0, concat_axis=0, tiled=True)  39.3 us
    all_to_all x1, starting transfers between devices, body(): lax.all_to_all(doc_grads, 'label', split_axis=0, concat_axis=0, tiled=True)  24.8 us
  transfers between devices with their start and end apart: 3, of which 3 were waited for; matrix products, arithmetic and copies ran while one was open for 1% of the time, Pallas kernels for 0%

commit v1 on v0

v1 whole, which is shorter than its diff:
```python
import jax
import jax.numpy as jnp
from jax import lax
from jax.sharding import Mesh, PartitionSpec as P

DOC_BLK = 256
LAB_BLK = 128
POS = 8
SCALE = 16.0

AXES = ("yh", "zp", "zb", "x", "yl", "c")
SIZES = (2, 16, 2, 4, 2, 2)
PLANE = ("yh", "x", "yl")


def unit_rows(matrix):
    widened = matrix.astype(jnp.float32)
    row_norm = jnp.sqrt(jnp.sum(widened * widened, axis=-1, keepdims=True) + 1e-06)
    return widened / row_norm, row_norm


def body(doc_emb, label_emb, short_blocks, short_len, positives):
    rows, width = doc_emb.shape
    yh, x, yl, core = (lax.axis_index(a) for a in ("yh", "x", "yl", "c"))
    depth = lax.axis_index(("zp", "zb"))
    plane = 16

    label_half = unit_rows(label_emb)[0].astype(jnp.bfloat16)
    pair = lax.all_gather(label_half, "zb", axis=0, tiled=True)

    own_unit, own_norm = unit_rows(doc_emb)
    own_pos = lax.dynamic_slice_in_dim(positives, ((x * 2 + yl) * 2 + core) * rows, rows, 0)
    packed = jnp.concatenate(
        [
            own_unit.astype(jnp.bfloat16),
            (own_pos // LAB_BLK).astype(jnp.bfloat16),
            (own_pos % LAB_BLK).astype(jnp.bfloat16),
            jnp.zeros((rows, 128 - 2 * POS), jnp.bfloat16),
        ],
        axis=1,
    )
    spread = jnp.broadcast_to(packed[None], (plane,) + packed.shape)
    docs = lax.all_to_all(spread, PLANE, split_axis=0, concat_axis=0, tiled=True)
    docs = docs.reshape(plane * rows, -1)

    own_labels = lax.all_gather(pair, "zp", axis=0, tiled=True)
    other_labels = lax.ppermute(own_labels, "c", [(0, 1), (1, 0)])
    labels = jnp.concatenate([own_labels, other_labels], axis=0)
    half = own_labels.shape[0]

    shard = (x * 2 + yl) * 2 + core
    first_own = shard * 8 + yh * 4
    first_other = (shard + 1 - 2 * core) * 8 + yh * 4
    grid = jnp.arange(4, dtype=jnp.int32)
    block_ids = jnp.concatenate([first_own + grid, first_other + grid])
    label_ids = (block_ids[:, None] * LAB_BLK + jnp.arange(LAB_BLK, dtype=jnp.int32)).reshape(-1)

    listed = short_blocks.reshape(2, 32, 4, 32)
    listed = lax.dynamic_index_in_dim(listed, depth, 1, keepdims=False).reshape(8, 32)
    list_len = lax.dynamic_index_in_dim(short_len.reshape(2, 32, 4), depth, 1, keepdims=False)
    list_len = list_len.reshape(8)
    in_list = jnp.arange(32, dtype=jnp.int32)[None, :] < list_len[:, None]
    active = jnp.any(
        (listed[:, :, None] == block_ids[None, None, :]) & in_list[:, :, None], axis=1
    ).astype(jnp.float32)

    doc_half = docs[:, :width]
    places = docs[:, width : width + 2 * POS].astype(jnp.float32)
    pos_ids = (places[:, :POS] * LAB_BLK + places[:, POS:]).astype(jnp.int32)
    scores = SCALE * lax.dot_general(
        doc_half, labels, (((1,), (1,)), ((), ())), preferred_element_type=jnp.float32
    )
    hit = jnp.zeros(scores.shape, jnp.bool_)
    for column in range(POS):
        hit = hit | (pos_ids[:, column][:, None] == label_ids[None, :])
    coef = SCALE * (jax.nn.sigmoid(scores) - hit.astype(jnp.float32))
    coef = (coef.reshape(8, 128, 8, LAB_BLK) * active[:, None, :, None]).reshape(1024, 1024)
    push = jnp.dot(coef.astype(jnp.bfloat16), labels, preferred_element_type=jnp.float32)
    pieces = lax.all_to_all(
        push.astype(jnp.bfloat16).reshape(plane, rows, width),
        PLANE,
        split_axis=0,
        concat_axis=0,
        tiled=True,
    )
    summed = jnp.sum(pieces.astype(jnp.float32), axis=0)
    radial = jnp.sum(summed * own_unit, axis=-1, keepdims=True)
    return (summed - radial * own_unit) / own_norm


def solution(mesh):
    fine = Mesh(mesh.devices.reshape(SIZES), AXES)
    doc, label = AXES[:3], AXES[3:]
    placed = (P(doc + label, None), P(label + doc, None), P(), P(), P(doc, None))
    return jax.shard_map(
        body, mesh=fine, in_specs=placed, out_specs=P(doc + label, None), check_vma=False
    )
```

time: 414 us -> 125 us (0.30)
  waiting for transfers between devices: 356 us -> 0.01 us
  blocking collectives: 0 us -> 82.6 us
  between operations: 13.5 us -> 0.16 us
  local copies, waits for them, and re-layouts: 2.35 us -> 9.7 us
  starting transfers between devices: 24.8 us -> 17.6 us
    all_gather x2 -> x0, waiting for transfers between devices: 316 us -> none  [the longest x1 256 us: body(): panels = lax.all_gather(label_emb, 'doc', axis=0, tiled=True)]
    all_gather x0 -> x2, blocking collectives: none -> 53.3 us  [the longest x1 49.8 us: body(): own_labels = lax.all_gather(pair, 'zp', axis=0, tiled=True)]
    all_to_all x1, waiting for transfers between devices: 39.3 us -> 0.01 us  [body(): lax.all_to_all(spread, PLANE, split_axis=0, concat_axis=0, tiled=True)]
    all_to_all x0 -> x1, blocking collectives: none -> 29.3 us  [body(): lax.all_to_all(push.astype(jnp.bfloat16).reshape(plane, rows, width), PLA...]
    all_to_all x1, starting transfers between devices: 24.8 us -> 7.58 us  [body(): lax.all_to_all(spread, PLANE, split_axis=0, concat_axis=0, tiled=True)]
    ppermute x0 -> x1, starting transfers between devices: none -> 10 us  [body(): other_labels = lax.ppermute(own_labels, 'c', [(0, 1), (1, 0)])]
    dot_general x2 -> x1, matrix products: 9 us -> 9.81 us  [body(): jnp.dot(coef.astype(jnp.bfloat16), labels, preferred_element_type=jnp.flo...]
  transfers between devices with their start and end apart: 3 -> 2, of which waited for: 3 -> 0; matrix products, arithmetic and copies ran while one was open for 1% -> 3% of each run, Pallas kernels for 0% -> 0%
where the time goes in v1:
time: 125 us; the launch traced here: 124 us
  blocking collectives  82.6 us (66%)
  starting transfers between devices  17.6 us (14%)
  matrix products  9.81 us (8%)
  local copies, waits for them, and re-layouts  9.7 us (8%)
  other arithmetic  4.29 us (3%)
    all_gather x1, blocking collectives, body(): own_labels = lax.all_gather(pair, 'zp', axis=0, tiled=True)  49.8 us
    all_to_all x1, blocking collectives, body(): lax.all_to_all(push.astype(jnp.bfloat16).reshape(plane, rows, width), PLA...  29.3 us
    ppermute x1, starting transfers between devices, body(): other_labels = lax.ppermute(own_labels, 'c', [(0, 1), (1, 0)])  10 us
    dot_general x1, matrix products, body(): jnp.dot(coef.astype(jnp.bfloat16), labels, preferred_element_type=jnp.flo...  9.81 us
    all_to_all x1, starting transfers between devices, body(): lax.all_to_all(spread, PLANE, split_axis=0, concat_axis=0, tiled=True)  7.58 us
    all_gather x1, blocking collectives, body(): pair = lax.all_gather(label_half, 'zb', axis=0, tiled=True)  3.5 us
  transfers between devices with their start and end apart: 2, of which 0 were waited for; matrix products, arithmetic and copies ran while one was open for 3% of the time, Pallas kernels for 0%

profile of v1, /device:TPU:1, one launch (start us, length us, event | category | flops | bytes accessed | tf_op | source)
XLA Modules:
  0.0 124.2 jit_solution(14414289369300842448)
XLA Ops:
  0.0 0.0 copy-start
  0.0 0.0 copy-start.2
  0.0 1.0 fusion.5
  1.0 0.0 copy-done
  1.1 0.1 constant_dynamic-slice_fusion.1
  1.1 0.1 copy.14
  1.3 1.0 fusion.14
  2.3 0.1 pad.5.clone
  2.3 0.1 maximum_maximum_fusion
  2.4 0.0 copy-start.4
  2.4 0.0 copy-start.3
  2.4 1.5 %broadcast_in_dim.5 = bf16[16,64,896]{2,1,0:T(8,128)(2,1)} broadcast(bf16[64,896]{1,0:T(8,128)(2,1)S(1)} %maximum_maximum_fusion), dimensions={1,2} | broadcast | bytes 1949696 | tf_op jit(solution)/shard_map/broadcast_in_dim | solution.py:42
  3.9 7.6 %all-to-all-start = ((bf16[16,64,896]{2,1,0:T(8,128)(2,1)}), bf16[16,64,896]{2,1,0:T(8,128)(2,1)S(1)}, u32[]{:S(2)}, u32[]{:S(2)}) async-start(bf16[16,64,896]{2,1,0:T(8,128)(2,1)} %broadcast_in_dim.5), calls=%async_computation | async-start | bytes 3670016 | tf_op jit(solution)/shard_map/all_to_all | solution.py:43
  11.5 0.0 copy-done.2
  11.5 0.1 fusion.6
  11.7 0.1 fusion.7
  11.8 3.5 %all_gather.6 = bf16[32,768]{1,0:T(8,128)(2,1)S(1)} all-gather(bf16[16,768]{1,0:T(8,128)(2,1)S(1)} %fusion.7), channel_id=1, replica_groups=mesh['yh'=2,'zp'=16,'zb'=2,'x'=4,'yl'=2,'c'=2] {'zb'}, dimensions={0}, use_global_device_ids=true | all-gather | bytes 73728 | tf_op jit(solution)/shard_map/all_gather | solution.py:29
  15.3 49.8 %all_gather.7 = bf16[512,768]{1,0:T(8,128)(2,1)S(1)} all-gather(bf16[32,768]{1,0:T(8,128)(2,1)S(1)} %all_gather.6), channel_id=1, replica_groups=mesh['yh'=2,'zp'=16,'zb'=2,'x'=4,'yl'=2,'c'=2] {'zp'}, dimensions={0}, use_global_device_ids=true | all-gather | bytes 835584 | tf_op jit(solution)/shard_map/all_gather | solution.py:46
  65.1 10.0 %collective-permute-start = (bf16[512,768]{1,0:T(8,128)(2,1)S(1)}, bf16[512,768]{1,0:T(8,128)(2,1)S(1)}, u32[]{:S(2)}, u32[]{:S(2)}) collective-permute-start(bf16[512,768]{1,0:T(8,128)(2,1)S(1)} %all_gather.7), channel_id=1, source_target_pairs={{0,1},{1,0},{2,3},{3,2},{4,5},{5,4},{6,7},{7,6},{8,9},{9,8},{10,11... | collective-permute-start | bytes 2359304 | tf_op jit(solution)/shard_map/ppermute | solution.py:47
  75.1 0.0 copy-done.4
  75.1 0.1 reshape.90
  75.2 0.1 lt.38
  75.3 0.0 copy-done.3
  75.3 0.8 copy.13
  76.1 0.7 constant_dynamic-slice_fusion
  76.8 0.1 broadcast_multiply_fusion
  76.8 0.1 iota_compare_fusion
  76.9 0.3 and_reduce_fusion
  77.2 0.9 constant_dynamic-update-slice_fusion.1
  78.2 0.1 add_bitcast_fusion
  78.2 0.0 collective-permute-done
  78.2 1.0 constant_dynamic-update-slice_fusion
  79.2 0.0 all-to-all-done
  79.2 0.2 fusion.4
  79.4 2.1 %slice_reduce_fusion.7 = (s32[1024]{0:T(1024)S(1)}, s32[1024]{0:T(1024)S(1)}, s32[1024]{0:T(1024)S(1)}, s32[1024]{0:T(1024)S(1)}, s32[1024]{0:T(1024)S(1)}, /*in...) fusion(s32[1024,8]{1,0:T(8,128)S(1)} %fusion.4), kind=kLoop, calls=%fused_computation.12 | loop fusion | bytes 65536 | tf_op jit(solution)/shard_map/slice | solution.py:75
  81.6 2.3 %mul.90 = f32[8,128,8,128]{3,2,1,0:T(8,128)} broadcast(f32[8,8]{1,0:T(8,128)S(1)} %convert_element_type.52), dimensions={0,2} | broadcast | bytes 4194560 | tf_op jit(solution)/shard_map/mul | solution.py:77
  83.8 9.8 %convolution_convert_fusion = bf16[1024,768]{1,0:T(8,128)(2,1)S(1)} fusion(bf16[1024,768]{1,0:T(8,128)(2,1)} %constant_dynamic-update-slice_fusion, f32[128,8,8,128]{3,2,1,0:T(8,128)} %bitcast.16, s32[1024]{0:T(1024)S(1)} %add_bitcast_fusion, s32[1024]{0:T(1024)S(1)} %get-tuple-element.6, s32[1024]{0:T(1024)S(1)} %get-tuple-element.7, ...), kind=kOutput, calls=%fused_computation.3 | convolution fusion | flops 3247177728 | bytes 10522624 | tf_op jit(solution)/shard_map/dot_general | solution.py:78
  93.6 0.0 copy-start.1
  93.7 29.3 %all_to_all.10 = bf16[16,64,768]{2,1,0:T(8,128)(2,1)S(1)} all-to-all(bf16[16,64,768]{2,1,0:T(8,128)(2,1)S(1)} %bitcast.19), channel_id=1, replica_groups=mesh['yh'=2,'zp'=16,'zb'=2,'x'=4,'yl'=2,'c'=2] {'yh','x','yl'}, dimensions={0} | all-to-all | bytes 3145728 | tf_op jit(solution)/shard_map/all_to_all | solution.py:79
  123.0 0.2 convert_reduce_fusion
  123.2 0.0 copy-done.1
  123.2 0.2 multiply_reduce_fusion
  123.4 0.8 subtract_divide_fusion
  (8 shorter events, 0.1 us)
Async XLA Ops:
  0.0 1.0 copy-start
  0.0 11.5 %copy-start.2 = (bf16[16,768]{1,0:T(8,128)(2,1)S(1)}, bf16[16,768]{1,0:T(8,128)(2,1)}, u32[]{:S(2)}) copy-start(bf16[16,768]{1,0:T(8,128)(2,1)} %param.6) | copy-start | bytes 73732
  2.4 72.7 %copy-start.4 = (s32[256]{0:T(256)S(1)}, s32[256]{0:T(256)}, u32[]{:S(2)}) copy-start(s32[256]{0:T(256)} %param.8) | copy-start | bytes 3076
  2.4 72.9 %copy-start.3 = (s32[256,32]{0,1:T(8,128)S(1)}, s32[256,32]{0,1:T(8,128)}, u32[]{:S(2)}) copy-start(s32[256,32]{0,1:T(8,128)} %param.7) | copy-start | bytes 98308
  3.9 75.3 %all-to-all-start = ((bf16[16,64,896]{2,1,0:T(8,128)(2,1)}), bf16[16,64,896]{2,1,0:T(8,128)(2,1)S(1)}, u32[]{:S(2)}, u32[]{:S(2)}) async-start(bf16[16,64,896]{2,1,0:T(8,128)(2,1)} %broadcast_in_dim.5), calls=%async_computation | async-start | bytes 3670016 | tf_op jit(solution)/shard_map/all_to_all | solution.py:43
  65.1 13.2 %collective-permute-start = (bf16[512,768]{1,0:T(8,128)(2,1)S(1)}, bf16[512,768]{1,0:T(8,128)(2,1)S(1)}, u32[]{:S(2)}, u32[]{:S(2)}) collective-permute-start(bf16[512,768]{1,0:T(8,128)(2,1)S(1)} %all_gather.7), channel_id=1, source_target_pairs={{0,1},{1,0},{2,3},{3,2},{4,5},{5,4},{6,7},{7,6},{8,9},{9,8},{10,11... | collective-permute-start | bytes 2359304 | tf_op jit(solution)/shard_map/ppermute | solution.py:47
  93.6 29.5 %copy-start.1 = (bf16[64,768]{1,0:T(8,128)(2,1)S(1)}, bf16[64,768]{1,0:T(8,128)(2,1)}, u32[]{:S(2)}) copy-start(bf16[64,768]{1,0:T(8,128)(2,1)} %param.5) | copy-start | bytes 294916

commit v2 on v1

v2 whole, which is shorter than its diff:
```python
import jax
import jax.numpy as jnp
from jax import lax
from jax.experimental import pallas as pl
from jax.experimental.pallas import tpu as pltpu
from jax.sharding import Mesh, PartitionSpec as P

DOC_BLK = 256
LAB_BLK = 128
POS = 8
SCALE = 16.0

AXES = ("yh", "zp", "zb", "x", "yl", "c")
SIZES = (2, 16, 2, 4, 2, 2)
PLANE = ("yh", "x", "yl")


def unit_rows(matrix):
    widened = matrix.astype(jnp.float32)
    row_norm = jnp.sqrt(jnp.sum(widened * widened, axis=-1, keepdims=True) + 1e-06)
    return widened / row_norm, row_norm


def push_kernel(live_ref, docs_ref, own_ref, other_ref, out_ref, total):
    yh, x, yl, core = (lax.axis_index(a) for a in ("yh", "x", "yl", "c"))
    depth = lax.axis_index("zp") * 2 + lax.axis_index("zb")
    width = own_ref.shape[1]
    shard = (x * 2 + yl) * 2 + core
    firsts = (shard * 8 + yh * 4, (shard + 1 - 2 * core) * 8 + yh * 4)
    lane = lax.broadcasted_iota(jnp.int32, (1, 2 * LAB_BLK), 1)
    upper = lane >= LAB_BLK

    @pl.loop(0, 8)
    def _(run):
        rows = pl.ds(pl.multiple_of(run * 128, 128), 128)
        column = (run // 4) * 128 + depth * 4 + run % 4
        total[...] = jnp.zeros_like(total)
        for side, labels_ref in ((0, own_ref), (1, other_ref)):
            live = [live_ref[side * 4 + i, column] for i in range(4)]
            count = live[0] + live[1] + live[2] + live[3]
            low = jnp.where(live[0] > 0, 0, jnp.where(live[1] > 0, 1, jnp.where(live[2] > 0, 2, 3)))
            high = jnp.where(live[3] > 0, 3, jnp.where(live[2] > 0, 2, jnp.where(live[1] > 0, 1, 0)))

            @pl.when(count > 0)
            def _():
                panel = jnp.concatenate(
                    [
                        labels_ref[pl.ds(pl.multiple_of(b * LAB_BLK, LAB_BLK), LAB_BLK), :]
                        for b in (low, high)
                    ],
                    axis=0,
                )
                scores = SCALE * lax.dot_general(
                    docs_ref[rows, :width],
                    panel,
                    (((1,), (1,)), ((), ())),
                    preferred_element_type=jnp.float32,
                )
                places = docs_ref[rows, width:].astype(jnp.float32)
                pos_ids = places[:, :POS] * LAB_BLK + places[:, POS : 2 * POS]
                ids = (firsts[side] + jnp.where(upper, high - 1, low)) * LAB_BLK + lane
                ids = ids.astype(jnp.float32)
                hit = pos_ids[:, 0:1] == ids
                for k in range(1, POS):
                    hit = hit | (pos_ids[:, k : k + 1] == ids)
                coef = SCALE * (jax.nn.sigmoid(scores) - jnp.where(hit, 1.0, 0.0))
                coef = jnp.where(upper & (count < 2), 0.0, coef)
                total[...] += jnp.dot(
                    coef.astype(jnp.bfloat16), panel, preferred_element_type=jnp.float32
                )

        out_ref[rows, :] = total[...].astype(jnp.bfloat16)


def body(doc_emb, label_emb, short_blocks, short_len, positives):
    rows, width = doc_emb.shape
    yh, x, yl, core = (lax.axis_index(a) for a in ("yh", "x", "yl", "c"))
    plane = 16

    label_half = unit_rows(label_emb)[0].astype(jnp.bfloat16)
    pair = lax.all_gather(label_half, "zb", axis=0, tiled=True)

    own_unit, own_norm = unit_rows(doc_emb)
    own_pos = lax.dynamic_slice_in_dim(positives, ((x * 2 + yl) * 2 + core) * rows, rows, 0)
    packed = jnp.concatenate(
        [
            own_unit.astype(jnp.bfloat16),
            (own_pos // LAB_BLK).astype(jnp.bfloat16),
            (own_pos % LAB_BLK).astype(jnp.bfloat16),
            jnp.zeros((rows, 128 - 2 * POS), jnp.bfloat16),
        ],
        axis=1,
    )
    spread = jnp.broadcast_to(packed[None], (plane,) + packed.shape)
    docs = lax.all_to_all(spread, PLANE, split_axis=0, concat_axis=0, tiled=True)
    docs = docs.reshape(plane * rows, -1)

    own_labels = lax.all_gather(pair, "zp", axis=0, tiled=True)
    other_labels = lax.ppermute(own_labels, "c", [(0, 1), (1, 0)])

    shard = (x * 2 + yl) * 2 + core
    grid = jnp.arange(4, dtype=jnp.int32)
    block_ids = yh * 4 + jnp.concatenate([shard * 8 + grid, (shard + 1 - 2 * core) * 8 + grid])
    slot = jnp.arange(short_blocks.shape[1], dtype=jnp.int32)
    live = jnp.any(
        (short_blocks.T[None] == block_ids[:, None, None])
        & (slot[:, None] < short_len[None, :])[None],
        axis=1,
    ).astype(jnp.int32)

    push = pl.pallas_call(
        push_kernel,
        out_shape=jax.ShapeDtypeStruct((plane * rows, width), jnp.bfloat16),
        in_specs=[pl.BlockSpec(memory_space=pltpu.SMEM)]
        + [pl.BlockSpec(memory_space=pltpu.VMEM)] * 3,
        out_specs=pl.BlockSpec(memory_space=pltpu.VMEM),
        scratch_shapes=[pltpu.VMEM((128, width), jnp.float32)],
        compiler_params=pltpu.CompilerParams(vmem_limit_bytes=32 * 2**20),
    )(live, docs, own_labels, other_labels)
    pieces = lax.all_to_all(
        push.reshape(plane, rows, width),
        PLANE,
        split_axis=0,
        concat_axis=0,
        tiled=True,
    )
    summed = jnp.sum(pieces.astype(jnp.float32), axis=0)
    radial = jnp.sum(summed * own_unit, axis=-1, keepdims=True)
    return (summed - radial * own_unit) / own_norm


def solution(mesh):
    fine = Mesh(mesh.devices.reshape(SIZES), AXES)
    doc, label = AXES[:3], AXES[3:]
    placed = (P(doc + label, None), P(label + doc, None), P(), P(), P(doc, None))
    return jax.shard_map(
        body, mesh=fine, in_specs=placed, out_specs=P(doc + label, None), check_vma=False
    )
```

time: 125 us -> 114 us (0.912)
  matrix products: 9.81 us -> 0 us
  local copies, waits for them, and re-layouts: 9.7 us -> 2.52 us
  Pallas kernels: 0 us -> 6.06 us
  waiting for transfers between devices: 0.01 us -> 1.62 us
  blocking collectives: 82.6 us -> 81.1 us
    dot_general x1 -> x0, matrix products: 9.81 us -> none  [body(): jnp.dot(coef.astype(jnp.bfloat16), labels, preferred_element_type=jnp.flo...]
    pallas_call x0 -> x1, Pallas kernels: none -> 6.06 us  [body(): pl.pallas_call(push_kernel, out_shape=jax.ShapeDtypeStruct((plane * rows,...]
    mul x1 -> x0, local copies, waits for them, and re-layouts: 2.26 us -> none  [body(): coef.reshape(8, 128, 8, LAB_BLK) * active[:, None, :, None]]
    slice x1 -> x0, local copies, waits for them, and re-layouts: 2.12 us -> none  [body(): hit = hit | (pos_ids[:, column][:, None] == label_ids[None, :])]
    ppermute x1, waiting for transfers between devices: 0.01 us -> 1.62 us  [body(): other_labels = lax.ppermute(own_labels, 'c', [(0, 1), (1, 0)])]
    all_to_all x1, blocking collectives: 29.3 us -> 27.8 us  [body(): lax.all_to_all(push.reshape(plane, rows, width), PLANE, split_axis=0, con...]
  transfers between devices with their start and end apart: 2 -> 2, of which waited for: 0 -> 1; matrix products, arithmetic and copies ran while one was open for 3% -> 0% of each run, Pallas kernels for 0% -> 0%
where the time goes in v2:
time: 114 us; the launch traced here: 113 us
  blocking collectives  81.1 us (71%)
  starting transfers between devices  17.7 us (16%)
  Pallas kernels  6.06 us (5%)
  other arithmetic  3.77 us (3%)
  local copies, waits for them, and re-layouts  2.52 us (2%)
  waiting for transfers between devices  1.62 us (1%)
    all_gather x1, blocking collectives, body(): own_labels = lax.all_gather(pair, 'zp', axis=0, tiled=True)  49.8 us
    all_to_all x1, blocking collectives, body(): lax.all_to_all(push.reshape(plane, rows, width), PLANE, split_axis=0, con...  27.8 us
    ppermute x1, starting transfers between devices, body(): other_labels = lax.ppermute(own_labels, 'c', [(0, 1), (1, 0)])  10 us
    all_to_all x1, starting transfers between devices, body(): lax.all_to_all(spread, PLANE, split_axis=0, concat_axis=0, tiled=True)  7.72 us
    pallas_call x1, Pallas kernels, body(): pl.pallas_call(push_kernel, out_shape=jax.ShapeDtypeStruct((plane * rows,...  6.06 us
    all_gather x1, blocking collectives, body(): pair = lax.all_gather(label_half, 'zb', axis=0, tiled=True)  3.5 us
  transfers between devices with their start and end apart: 2, of which 1 were waited for; matrix products, arithmetic and copies ran while one was open for 0% of the time, Pallas kernels for 0%

profile of v2, /device:TPU:1, one launch (start us, length us, event | category | flops | bytes accessed | tf_op | source)
XLA Modules:
  0.0 113.0 jit_solution(8189237641816250395)
XLA Ops:
  0.0 0.0 copy-start
  0.0 0.8 copy-done
  0.8 0.1 constant_dynamic-slice_fusion
  0.8 0.1 copy.8
  1.0 1.0 fusion
  2.0 1.0 fusion.7
  3.0 0.1 pad.3.clone
  3.1 0.1 maximum_maximum_fusion
  3.2 1.5 %broadcast_in_dim.5 = bf16[16,64,896]{2,1,0:T(8,128)(2,1)} broadcast(bf16[64,896]{1,0:T(8,128)(2,1)S(1)} %maximum_maximum_fusion), dimensions={1,2} | broadcast | bytes 1949696 | tf_op jit(solution)/shard_map/broadcast_in_dim | solution.py:94
  4.7 0.0 copy-start.2
  4.7 0.0 copy-start.4
  4.7 0.0 copy-start.3
  4.7 7.7 %all-to-all-start = ((bf16[16,64,896]{2,1,0:T(8,128)(2,1)}), bf16[16,64,896]{2,1,0:T(8,128)(2,1)S(1)}, u32[]{:S(2)}, u32[]{:S(2)}) async-start(bf16[16,64,896]{2,1,0:T(8,128)(2,1)} %broadcast_in_dim.5), calls=%async_computation | async-start | bytes 3670016 | tf_op jit(solution)/shard_map/all_to_all | solution.py:95
  12.4 0.0 copy-done.2
  12.4 0.1 fusion.1
  12.5 0.1 fusion.2
  12.6 3.5 %all_gather.6 = bf16[32,768]{1,0:T(8,128)(2,1)S(1)} all-gather(bf16[16,768]{1,0:T(8,128)(2,1)S(1)} %fusion.2), channel_id=1, replica_groups=mesh['yh'=2,'zp'=16,'zb'=2,'x'=4,'yl'=2,'c'=2] {'zb'}, dimensions={0}, use_global_device_ids=true | all-gather | bytes 73728 | tf_op jit(solution)/shard_map/all_gather | solution.py:81
  16.1 49.8 %all_gather.7.own_ref = bf16[512,768]{1,0:T(8,128)(2,1)S(1)} all-gather(bf16[32,768]{1,0:T(8,128)(2,1)S(1)} %all_gather.6), channel_id=1, replica_groups=mesh['yh'=2,'zp'=16,'zb'=2,'x'=4,'yl'=2,'c'=2] {'zp'}, dimensions={0}, use_global_device_ids=true | all-gather | bytes 835584 | tf_op jit(solution)/shard_map/all_gather | solution.py:98
  65.9 10.0 %collective-permute-start = (bf16[512,768]{1,0:T(8,128)(2,1)S(1)}, bf16[512,768]{1,0:T(8,128)(2,1)S(1)}, u32[]{:S(2)}, u32[]{:S(2)}) collective-permute-start(bf16[512,768]{1,0:T(8,128)(2,1)S(1)} %all_gather.7.own_ref), channel_id=1, source_target_pairs={{0,1},{1,0},{2,3},{3,2},{4,5},{5,4},{6,7},{7,6},{8,9},{9,8},{10,11... | collective-permute-start | bytes 2359304 | tf_op jit(solution)/shard_map/ppermute | solution.py:99
  76.0 0.1 add_add_fusion
  76.0 0.0 copy-done.4
  76.1 0.0 copy-done.3
  76.1 0.1 and_reduce_fusion
  76.2 1.6 %collective-permute-done.other_ref = bf16[512,768]{1,0:T(8,128)(2,1)S(1)} collective-permute-done((bf16[512,768]{1,0:T(8,128)(2,1)S(1)}, bf16[512,768]{1,0:T(8,128)(2,1)S(1)}, u32[]{:S(2)}, u32[]{:S(2)}) %collective-permute-start) | collective-permute-done | bytes 786464 | tf_op jit(solution)/shard_map/ppermute | solution.py:99
  77.8 0.0 all-to-all-done
  77.8 6.1 %shard_map.55 = bf16[1024,768]{1,0:T(8,128)(2,1)S(1)} custom-call(s32[8,256]{1,0:T(8,128)S(1)} %convert_element_type.24.live_ref, bf16[1024,896]{1,0:T(8,128)(2,1)S(1)} %bitcast.3, bf16[512,768]{1,0:T(8,128)(2,1)S(1)} %all_gather.7.own_ref, bf16[512,768]{1,0:T(8,128)(2,1)S(1)} %collective-permute-done.other_ref), custom_call_target="tpu_custom_call" | custom-call | tf_op jit(solution)/shard_map/pallas_call | solution.py:111
  83.9 0.0 copy-start.1
  83.9 27.8 %all_to_all.10 = bf16[16,64,768]{2,1,0:T(8,128)(2,1)S(1)} all-to-all(bf16[16,64,768]{2,1,0:T(8,128)(2,1)S(1)} %bitcast.4), channel_id=1, replica_groups=mesh['yh'=2,'zp'=16,'zb'=2,'x'=4,'yl'=2,'c'=2] {'yh','x','yl'}, dimensions={0} | all-to-all | bytes 3145728 | tf_op jit(solution)/shard_map/all_to_all | solution.py:120
  111.8 0.2 convert_reduce_fusion
  112.0 0.0 copy-done.1
  112.0 0.2 multiply_reduce_fusion
  112.2 0.8 subtract_divide_fusion
  (7 shorter events, 0.1 us)
Async XLA Ops:
  0.0 0.8 copy-start
  4.7 7.7 %copy-start.2 = (bf16[16,768]{1,0:T(8,128)(2,1)S(1)}, bf16[16,768]{1,0:T(8,128)(2,1)}, u32[]{:S(2)}) copy-start(bf16[16,768]{1,0:T(8,128)(2,1)} %param.6) | copy-start | bytes 73732
  4.7 71.4 %copy-start.4 = (s32[256]{0:T(256)S(1)}, s32[256]{0:T(256)}, u32[]{:S(2)}) copy-start(s32[256]{0:T(256)} %param.8) | copy-start | bytes 3076
  4.7 71.4 %copy-start.3 = (s32[256,32]{0,1:T(8,128)S(1)}, s32[256,32]{0,1:T(8,128)}, u32[]{:S(2)}) copy-start(s32[256,32]{0,1:T(8,128)} %param.7) | copy-start | bytes 98308
  4.7 73.2 %all-to-all-start = ((bf16[16,64,896]{2,1,0:T(8,128)(2,1)}), bf16[16,64,896]{2,1,0:T(8,128)(2,1)S(1)}, u32[]{:S(2)}, u32[]{:S(2)}) async-start(bf16[16,64,896]{2,1,0:T(8,128)(2,1)} %broadcast_in_dim.5), calls=%async_computation | async-start | bytes 3670016 | tf_op jit(solution)/shard_map/all_to_all | solution.py:95
  65.9 11.9 %collective-permute-start = (bf16[512,768]{1,0:T(8,128)(2,1)S(1)}, bf16[512,768]{1,0:T(8,128)(2,1)S(1)}, u32[]{:S(2)}, u32[]{:S(2)}) collective-permute-start(bf16[512,768]{1,0:T(8,128)(2,1)S(1)} %all_gather.7.own_ref), channel_id=1, source_target_pairs={{0,1},{1,0},{2,3},{3,2},{4,5},{5,4},{6,7},{7,6},{8,9},{9,8},{10,11... | collective-permute-start | bytes 2359304 | tf_op jit(solution)/shard_map/ppermute | solution.py:99
  83.9 28.1 %copy-start.1 = (bf16[64,768]{1,0:T(8,128)(2,1)S(1)}, bf16[64,768]{1,0:T(8,128)(2,1)}, u32[]{:S(2)}) copy-start(bf16[64,768]{1,0:T(8,128)(2,1)} %param.5) | copy-start | bytes 294916

commit v3 on v1

v3 whole, which is shorter than its diff:
```python
import functools

import jax
import jax.numpy as jnp
from jax import lax
from jax.experimental import pallas as pl
from jax.experimental.pallas import tpu as pltpu
from jax.sharding import Mesh, PartitionSpec as P

LAB_BLK = 128
POS = 8
SCALE = 16.0
RUN = 128
RUNS = 8

AXES = ("yh", "zp", "zb", "x", "yl", "c")
SIZES = (2, 16, 2, 4, 2, 2)
PLANE = ("yh", "x", "yl")
PLANE_SIZE = 16


def unit_rows(matrix):
    widened = matrix.astype(jnp.float32)
    row_norm = jnp.sqrt(jnp.sum(widened * widened, axis=-1, keepdims=True) + 1e-06)
    return widened / row_norm, row_norm


def place():
    return tuple(lax.axis_index(a) for a in AXES)


def first_blocks():
    yh, _, _, x, yl, core = place()
    shard = (x * 2 + yl) * 2 + core
    return shard * 8 + yh * 4, (shard + 1 - 2 * core) * 8 + yh * 4


def prepare_kernel(doc_ref, label_ref, pos_ref, half_ref, spread_ref, packed, sems):
    half_ref[...] = unit_rows(label_ref[...])[0].astype(jnp.bfloat16)
    rows, width = doc_ref.shape
    packed[:, :width] = unit_rows(doc_ref[...])[0].astype(jnp.bfloat16)
    _, _, _, x, yl, core = place()
    ids = pos_ref[:, pl.ds(pl.multiple_of((x * 2 + yl) * 128, 128), 128)]
    parts = jnp.concatenate(
        [
            (ids // LAB_BLK).astype(jnp.float32),
            (ids % LAB_BLK).astype(jnp.float32),
            jnp.zeros((128 - 2 * POS, 128), jnp.float32),
        ],
        axis=0,
    )
    parts = parts.T
    packed[:, width:] = jnp.where(core == 0, parts[:rows], parts[rows:]).astype(jnp.bfloat16)
    copies = [
        pltpu.make_async_copy(packed, spread_ref.at[i], sems.at[i]) for i in range(PLANE_SIZE)
    ]
    for copy in copies:
        copy.start()
    for copy in copies:
        copy.wait()


def push_kernel(side, live_ref, docs_ref, labels_ref, *refs):
    before_ref, out_ref, tasks = refs if side else (None, *refs)
    _, zp, zb, _, _, _ = place()
    width = labels_ref.shape[1]
    first = first_blocks()[side]
    lane = lax.broadcasted_iota(jnp.int32, (1, 2 * LAB_BLK), 1)
    upper = lane >= LAB_BLK
    offset = (lane % LAB_BLK) ^ (16 * zb)

    number = jnp.int32(0)
    for run in range(RUNS):
        column = (run // 4) * 128 + (zp * 2 + zb) * 4 + run % 4
        live = [live_ref[side * 4 + i, column] for i in range(4)]
        count = live[0] + live[1] + live[2] + live[3]
        low = jnp.where(live[0] > 0, 0, jnp.where(live[1] > 0, 1, jnp.where(live[2] > 0, 2, 3)))
        high = jnp.where(live[3] > 0, 3, jnp.where(live[2] > 0, 2, jnp.where(live[1] > 0, 1, 0)))
        tasks[4 * number] = run
        tasks[4 * number + 1] = low
        tasks[4 * number + 2] = high
        tasks[4 * number + 3] = count
        number = number + jnp.where(count > 0, 1, 0)

        @pl.when(count == 0)
        def _():
            rows = pl.ds(run * RUN, RUN)
            if side:
                out_ref[rows, :] = before_ref[rows, :].astype(out_ref.dtype)
            else:
                out_ref[rows, :] = jnp.zeros((RUN, width), out_ref.dtype)

    def work(task):
        run, low, high, count = (tasks[4 * task + i] for i in range(4))
        rows = pl.ds(pl.multiple_of(run * RUN, RUN), RUN)
        panel = jnp.concatenate(
            [
                labels_ref[pl.ds(pl.multiple_of(b * LAB_BLK, LAB_BLK), LAB_BLK), :]
                for b in (low, high)
            ],
            axis=0,
        )
        scores = SCALE * lax.dot_general(
            docs_ref[rows, :width],
            panel,
            (((1,), (1,)), ((), ())),
            preferred_element_type=jnp.float32,
        )
        places = docs_ref[rows, width:].astype(jnp.float32)
        pos_ids = places[:, :POS] * LAB_BLK + places[:, POS : 2 * POS]
        ids = ((first + jnp.where(upper, high, low)) * LAB_BLK + offset).astype(jnp.float32)
        hit = pos_ids[:, 0:1] == ids
        for k in range(1, POS):
            hit = hit | (pos_ids[:, k : k + 1] == ids)
        coef = SCALE * (jax.nn.sigmoid(scores) - jnp.where(hit, 1.0, 0.0))
        coef = jnp.where(upper & (count < 2), 0.0, coef).astype(jnp.bfloat16)
        total = jnp.dot(coef, panel, preferred_element_type=jnp.float32)
        if side:
            total = total + before_ref[rows, :]
        return rows, total.astype(out_ref.dtype)

    @pl.loop(0, (number + 1) // 2)
    def _(pair):
        results = [work(2 * pair), work(jnp.minimum(2 * pair + 1, number - 1))]
        for rows, total in results:
            out_ref[rows, :] = total


def vmem(count):
    return [pl.BlockSpec(memory_space=pltpu.VMEM)] * count


def body(doc_emb, label_emb, short_blocks, short_len, positives):
    rows, width = doc_emb.shape
    label_half, spread = pl.pallas_call(
        prepare_kernel,
        out_shape=(
            jax.ShapeDtypeStruct(label_emb.shape, jnp.bfloat16),
            jax.ShapeDtypeStruct((PLANE_SIZE, rows, width + 128), jnp.bfloat16),
        ),
        in_specs=vmem(3),
        out_specs=(vmem(1)[0], pl.BlockSpec(memory_space=pl.ANY)),
        scratch_shapes=[
            pltpu.VMEM((rows, width + 128), jnp.bfloat16),
            pltpu.SemaphoreType.DMA((PLANE_SIZE,)),
        ],
    )(doc_emb, label_emb, positives.T)

    neighbour = lax.ppermute(label_half, "zb", [(0, 1), (1, 0)])
    docs = lax.all_to_all(spread, PLANE, split_axis=0, concat_axis=0, tiled=True)
    docs = docs.reshape(PLANE_SIZE * rows, width + 128)
    pair = jnp.concatenate([label_half, neighbour], axis=0)
    own_labels = lax.all_gather(pair, "zp", axis=0, tiled=True)
    other_labels = lax.ppermute(own_labels, "c", [(0, 1), (1, 0)])

    grid = jnp.arange(4, dtype=jnp.int32)
    block_ids = jnp.concatenate([first + grid for first in first_blocks()])
    slot = jnp.arange(short_blocks.shape[1], dtype=jnp.int32)
    live = jnp.any(
        (short_blocks.T[None] == block_ids[:, None, None])
        & (slot[:, None] < short_len[None, :])[None],
        axis=1,
    ).astype(jnp.int32)

    def push(side, dtype, *operands):
        return pl.pallas_call(
            functools.partial(push_kernel, side),
            out_shape=jax.ShapeDtypeStruct((RUNS * RUN, width), dtype),
            in_specs=[pl.BlockSpec(memory_space=pltpu.SMEM)] + vmem(len(operands)),
            out_specs=vmem(1)[0],
            scratch_shapes=[pltpu.SMEM((4 * RUNS + 4,), jnp.int32)],
            compiler_params=pltpu.CompilerParams(vmem_limit_bytes=32 * 2**20),
            cost_estimate=pl.CostEstimate(
                flops=4 * RUNS * RUN * 2 * LAB_BLK * width,
                bytes_accessed=6 * 2**20,
                transcendentals=2 * RUNS * RUN * 2 * LAB_BLK,
            ),
        )(live, *operands)

    part = push(0, jnp.float32, docs, own_labels)
    part = push(1, jnp.bfloat16, docs, other_labels, part)
    pieces = lax.all_to_all(
        part.reshape(PLANE_SIZE, rows, width), PLANE, split_axis=0, concat_axis=0, tiled=True
    )
    own_unit, own_norm = unit_rows(doc_emb)
    summed = jnp.sum(pieces.astype(jnp.float32), axis=0)
    radial = jnp.sum(summed * own_unit, axis=-1, keepdims=True)
    return (summed - radial * own_unit) / own_norm


def solution(mesh):
    fine = Mesh(mesh.devices.reshape(SIZES), AXES)
    doc, label = AXES[:3], AXES[3:]
    placed = (P(doc + label, None), P(label + doc, None), P(), P(), P(doc, None))
    return jax.shard_map(
        body, mesh=fine, in_specs=placed, out_specs=P(doc + label, None), check_vma=False
    )
```

time: 125 us -> 117 us (0.936)
  blocking collectives: 82.6 us -> 48.6 us
  waiting for transfers between devices: 0.01 us -> 25.7 us
  Pallas kernels: 0 us -> 12.1 us
  starting transfers between devices: 17.6 us -> 28.4 us
  matrix products: 9.81 us -> 0 us
  local copies, waits for them, and re-layouts: 9.7 us -> 0.02 us
  other arithmetic: 4.29 us -> 1.56 us
    all_to_all x1 -> x0, blocking collectives: 29.3 us -> none  [body(): lax.all_to_all(push.astype(jnp.bfloat16).reshape(plane, rows, width), PLA...]
    all_to_all x0 -> x1, waiting for transfers between devices: none -> 24.5 us  [body(): lax.all_to_all(part.reshape(PLANE_SIZE, rows, width), PLANE, split_axis=0...]
    pallas_call x0 -> x3, Pallas kernels: none -> 12.1 us  [the longest x2 8.99 us: push(): pl.pallas_call(functools.partial(push_kernel, side), out_shape=jax.ShapeD...]
    dot_general x1 -> x0, matrix products: 9.81 us -> none  [body(): jnp.dot(coef.astype(jnp.bfloat16), labels, preferred_element_type=jnp.flo...]
    all_to_all x0 -> x1, starting transfers between devices: none -> 5.79 us  [body(): lax.all_to_all(part.reshape(PLANE_SIZE, rows, width), PLANE, split_axis=0...]
    ppermute x0 -> x1, starting transfers between devices: none -> 3.55 us  [body(): neighbour = lax.ppermute(label_half, 'zb', [(0, 1), (1, 0)])]
    all_gather x1 -> x0, blocking collectives: 3.5 us -> none  [body(): pair = lax.all_gather(label_half, 'zb', axis=0, tiled=True)]
    mul x1 -> x0, local copies, waits for them, and re-layouts: 2.26 us -> none  [body(): coef.reshape(8, 128, 8, LAB_BLK) * active[:, None, :, None]]
  transfers between devices with their start and end apart: 2 -> 4, of which waited for: 0 -> 2; matrix products, arithmetic and copies ran while one was open for 3% -> 0% of each run, Pallas kernels for 0% -> 3%
where the time goes in v3:
time: 117 us; the launch traced here: 116 us
  blocking collectives  48.6 us (42%)
  starting transfers between devices  28.4 us (24%)
  waiting for transfers between devices  25.7 us (22%)
  Pallas kernels  12.1 us (10%)
  other arithmetic  1.56 us (1%)
    all_gather x1, blocking collectives, body(): own_labels = lax.all_gather(pair, 'zp', axis=0, tiled=True)  48.6 us
    all_to_all x1, waiting for transfers between devices, body(): lax.all_to_all(part.reshape(PLANE_SIZE, rows, width), PLANE, split_axis=0...  24.5 us
    ppermute x1, starting transfers between devices, body(): other_labels = lax.ppermute(own_labels, 'c', [(0, 1), (1, 0)])  11.3 us
    pallas_call x2, Pallas kernels, push(): pl.pallas_call(functools.partial(push_kernel, side), out_shape=jax.ShapeD...  8.99 us
    all_to_all x1, starting transfers between devices, body(): lax.all_to_all(spread, PLANE, split_axis=0, concat_axis=0, tiled=True)  7.73 us
    all_to_all x1, starting transfers between devices, body(): lax.all_to_all(part.reshape(PLANE_SIZE, rows, width), PLANE, split_axis=0...  5.79 us
    ppermute x1, starting transfers between devices, body(): neighbour = lax.ppermute(label_half, 'zb', [(0, 1), (1, 0)])  3.55 us
    pallas_call x1, Pallas kernels, body(): pl.pallas_call(prepare_kernel, out_shape=(jax.ShapeDtypeStruct(label_emb....  3.07 us
  transfers between devices with their start and end apart: 4, of which 2 were waited for; matrix products, arithmetic and copies ran while one was open for 0% of the time, Pallas kernels for 3%

profile of v3, /device:TPU:1, one launch (start us, length us, event | category | flops | bytes accessed | tf_op | source)
XLA Modules:
  0.0 116.5 jit_solution(13581613375725995439)
XLA Ops:
  0.0 3.1 %shard_map.55 = (bf16[16,768]{1,0:T(8,128)(2,1)}, bf16[16,64,896]{2,1,0:T(8,128)(2,1)}) custom-call(bf16[64,768]{1,0:T(8,128)(2,1)} %doc_ref.1, bf16[16,768]{1,0:T(8,128)(2,1)} %label_ref.1, s32[8,1024]{1,0:T(8,128)} %bitcast.6), custom_call_target="tpu_custom_call" | custom-call | tf_op jit(solution)/shard_map/pallas_call | solution.py:135
  3.1 0.0 copy-start.2
  3.1 0.0 copy-start.3
  3.1 0.0 copy-start.1
  3.1 7.7 %all-to-all-start = ((bf16[16,64,896]{2,1,0:T(8,128)(2,1)}), bf16[16,64,896]{2,1,0:T(8,128)(2,1)S(1)}, u32[]{:S(2)}, u32[]{:S(2)}) async-start(bf16[16,64,896]{2,1,0:T(8,128)(2,1)} %get-tuple-element.7), calls=%async_computation | async-start | bytes 3670016 | tf_op jit(solution)/shard_map/all_to_all | solution.py:150
  10.8 0.0 copy-done.2
  10.9 3.5 %collective-permute-start = (bf16[16,768]{1,0:T(8,128)(2,1)S(1)}, bf16[16,768]{1,0:T(8,128)(2,1)S(1)}, u32[]{:S(2)}, u32[]{:S(2)}) collective-permute-start(bf16[16,768]{1,0:T(8,128)(2,1)S(1)} %copy-done.2), channel_id=1, source_target_pairs={{0,16},{16,0},{1,17},{17,1},{2,18},{18,2},{3,19},{19,3},{4,20},{20... | collective-permute-start | bytes 73736 | tf_op jit(solution)/shard_map/ppermute | solution.py:149
  14.4 1.2 %collective-permute-done = bf16[16,768]{1,0:T(8,128)(2,1)S(1)} collective-permute-done((bf16[16,768]{1,0:T(8,128)(2,1)S(1)}, bf16[16,768]{1,0:T(8,128)(2,1)S(1)}, u32[]{:S(2)}, u32[]{:S(2)}) %collective-permute-start) | collective-permute-done | bytes 24608 | tf_op jit(solution)/shard_map/ppermute | solution.py:149
  15.6 48.6 %all_gather.3.labels_ref = bf16[512,768]{1,0:T(8,128)(2,1)S(1)} all-gather(bf16[32,768]{1,0:T(8,128)(2,1)S(1)} %pad_maximum_fusion), channel_id=1, replica_groups=mesh['yh'=2,'zp'=16,'zb'=2,'x'=4,'yl'=2,'c'=2] {'zp'}, dimensions={0}, use_global_device_ids=true | all-gather | bytes 835584 | tf_op jit(solution)/shard_map/all_gather | solution.py:153
  64.2 11.3 %collective-permute-start.1 = (bf16[512,768]{1,0:T(8,128)(2,1)S(1)}, bf16[512,768]{1,0:T(8,128)(2,1)S(1)}, u32[]{:S(2)}, u32[]{:S(2)}) collective-permute-start(bf16[512,768]{1,0:T(8,128)(2,1)S(1)} %all_gather.3.labels_ref), channel_id=1, source_target_pairs={{0,1},{1,0},{2,3},{3,2},{4,5},{5,4},{6,7},{7,6},{8,9},{9,8},{10,11... | collective-permute-start | bytes 2359304 | tf_op jit(solution)/shard_map/ppermute | solution.py:154
  75.5 0.1 pad_add_fusion
  75.6 0.0 copy-done.3
  75.6 0.0 copy-done.1
  75.6 0.1 and_reduce_fusion
  75.8 0.0 all-to-all-done
  75.8 3.9 %shard_map.56.refs_0_ = f32[1024,768]{1,0:T(8,128)S(1)} custom-call(s32[8,256]{1,0:T(8,128)S(1)} %convert_element_type.9.live_ref, bf16[1024,896]{1,0:T(8,128)(2,1)S(1)} %bitcast.4, bf16[512,768]{1,0:T(8,128)(2,1)S(1)} %all_gather.3.labels_ref), custom_call_target="tpu_custom_call" | custom-call | flops 805306368 | bytes 6291456 | tf_op jit(solution)/shard_map/pallas_call | solution.py:166
  79.7 0.0 collective-permute-done.1.labels_ref
  79.7 5.1 %shard_map.57 = bf16[1024,768]{1,0:T(8,128)(2,1)} custom-call(s32[8,256]{1,0:T(8,128)S(1)} %convert_element_type.9.live_ref, bf16[1024,896]{1,0:T(8,128)(2,1)S(1)} %bitcast.5, bf16[512,768]{1,0:T(8,128)(2,1)S(1)} %collective-permute-done.1.labels_ref, f32[1024,768]{1,0:T(8,128)S(1)} %shard_map.56.refs_0_), custom_call_target="tpu_custom_call" | custom-call | flops 805306368 | bytes 6291456 | tf_op jit(solution)/shard_map/pallas_call | solution.py:166
  84.8 0.0 copy-start
  84.8 5.8 %all-to-all-start.1 = ((bf16[16,64,768]{2,1,0:T(8,128)(2,1)}), bf16[16,64,768]{2,1,0:T(8,128)(2,1)S(1)}, u32[]{:S(2)}, u32[]{:S(2)}) async-start(bf16[16,64,768]{2,1,0:T(8,128)(2,1)} %bitcast.3), calls=%async_computation.1 | async-start | bytes 3145728 | tf_op jit(solution)/shard_map/all_to_all | solution.py:182
  90.6 0.0 copy-done
  90.6 0.1 fusion
  90.7 24.5 %all-to-all-done.1 = bf16[16,64,768]{2,1,0:T(8,128)(2,1)S(1)} async-done(((bf16[16,64,768]{2,1,0:T(8,128)(2,1)}), bf16[16,64,768]{2,1,0:T(8,128)(2,1)S(1)}, u32[]{:S(2)}, u32[]{:S(2)}) %all-to-all-start.1) | async-done | bytes 1572896 | tf_op jit(solution)/shard_map/all_to_all | solution.py:182
  115.2 0.2 convert_reduce_fusion
  115.5 0.2 multiply_reduce_fusion
  115.7 0.8 subtract_divide_fusion
  (5 shorter events, 0.0 us)
Async XLA Ops:
  3.1 7.8 %copy-start.2 = (bf16[16,768]{1,0:T(8,128)(2,1)S(1)}, bf16[16,768]{1,0:T(8,128)(2,1)}, u32[]{:S(2)}) copy-start(bf16[16,768]{1,0:T(8,128)(2,1)} %get-tuple-element.8) | copy-start | bytes 73732
  3.1 72.5 %copy-start.3 = (s32[256]{0:T(256)S(1)}, s32[256]{0:T(256)}, u32[]{:S(2)}) copy-start(s32[256]{0:T(256)} %param.8) | copy-start | bytes 3076
  3.1 72.5 %copy-start.1 = (s32[256,32]{0,1:T(8,128)S(1)}, s32[256,32]{0,1:T(8,128)}, u32[]{:S(2)}) copy-start(s32[256,32]{0,1:T(8,128)} %param.7) | copy-start | bytes 98308
  3.1 72.7 %all-to-all-start = ((bf16[16,64,896]{2,1,0:T(8,128)(2,1)}), bf16[16,64,896]{2,1,0:T(8,128)(2,1)S(1)}, u32[]{:S(2)}, u32[]{:S(2)}) async-start(bf16[16,64,896]{2,1,0:T(8,128)(2,1)} %get-tuple-element.7), calls=%async_computation | async-start | bytes 3670016 | tf_op jit(solution)/shard_map/all_to_all | solution.py:150
  10.9 4.8 %collective-permute-start = (bf16[16,768]{1,0:T(8,128)(2,1)S(1)}, bf16[16,768]{1,0:T(8,128)(2,1)S(1)}, u32[]{:S(2)}, u32[]{:S(2)}) collective-permute-start(bf16[16,768]{1,0:T(8,128)(2,1)S(1)} %copy-done.2), channel_id=1, source_target_pairs={{0,16},{16,0},{1,17},{17,1},{2,18},{18,2},{3,19},{19,3},{4,20},{20... | collective-permute-start | bytes 73736 | tf_op jit(solution)/shard_map/ppermute | solution.py:149
  64.2 15.5 %collective-permute-start.1 = (bf16[512,768]{1,0:T(8,128)(2,1)S(1)}, bf16[512,768]{1,0:T(8,128)(2,1)S(1)}, u32[]{:S(2)}, u32[]{:S(2)}) collective-permute-start(bf16[512,768]{1,0:T(8,128)(2,1)S(1)} %all_gather.3.labels_ref), channel_id=1, source_target_pairs={{0,1},{1,0},{2,3},{3,2},{4,5},{5,4},{6,7},{7,6},{8,9},{9,8},{10,11... | collective-permute-start | bytes 2359304 | tf_op jit(solution)/shard_map/ppermute | solution.py:154
  84.8 5.8 %copy-start = (bf16[64,768]{1,0:T(8,128)(2,1)S(1)}, bf16[64,768]{1,0:T(8,128)(2,1)}, u32[]{:S(2)}) copy-start(bf16[64,768]{1,0:T(8,128)(2,1)} %doc_ref.1) | copy-start | bytes 294916
  84.8 30.5 %all-to-all-start.1 = ((bf16[16,64,768]{2,1,0:T(8,128)(2,1)}), bf16[16,64,768]{2,1,0:T(8,128)(2,1)S(1)}, u32[]{:S(2)}, u32[]{:S(2)}) async-start(bf16[16,64,768]{2,1,0:T(8,128)(2,1)} %bitcast.3), calls=%async_computation.1 | async-start | bytes 3145728 | tf_op jit(solution)/shard_map/all_to_all | solution.py:182

commit v4 on v3

--- a/solution.py
+++ b/solution.py
@@ -67,7 +67,7 @@
     first = first_blocks()[side]
     lane = lax.broadcasted_iota(jnp.int32, (1, 2 * LAB_BLK), 1)
     upper = lane >= LAB_BLK
-    offset = (lane % LAB_BLK) ^ (16 * zb)
+    offset = lane % LAB_BLK
 
     number = jnp.int32(0)
     for run in range(RUNS):
@@ -126,6 +126,15 @@
             out_ref[rows, :] = total
 
 
+def finish_kernel(pieces_ref, doc_ref, out_ref):
+    summed = pieces_ref[0].astype(jnp.float32)
+    for i in range(1, PLANE_SIZE):
+        summed = summed + pieces_ref[i].astype(jnp.float32)
+    own_unit, own_norm = unit_rows(doc_ref[...])
+    radial = jnp.sum(summed * own_unit, axis=-1, keepdims=True)
+    out_ref[...] = (summed - radial * own_unit) / own_norm
+
+
 def vmem(count):
     return [pl.BlockSpec(memory_space=pltpu.VMEM)] * count
 
@@ -146,10 +155,9 @@
         ],
     )(doc_emb, label_emb, positives.T)
 
-    neighbour = lax.ppermute(label_half, "zb", [(0, 1), (1, 0)])
     docs = lax.all_to_all(spread, PLANE, split_axis=0, concat_axis=0, tiled=True)
     docs = docs.reshape(PLANE_SIZE * rows, width + 128)
-    pair = jnp.concatenate([label_half, neighbour], axis=0)
+    pair = lax.all_gather(label_half, "zb", axis=0, tiled=True)
     own_labels = lax.all_gather(pair, "zp", axis=0, tiled=True)
     other_labels = lax.ppermute(own_labels, "c", [(0, 1), (1, 0)])
 
@@ -182,10 +190,13 @@
     pieces = lax.all_to_all(
         part.reshape(PLANE_SIZE, rows, width), PLANE, split_axis=0, concat_axis=0, tiled=True
     )
-    own_unit, own_norm = unit_rows(doc_emb)
-    summed = jnp.sum(pieces.astype(jnp.float32), axis=0)
-    radial = jnp.sum(summed * own_unit, axis=-1, keepdims=True)
-    return (summed - radial * own_unit) / own_norm
+    return pl.pallas_call(
+        finish_kernel,
+        out_shape=jax.ShapeDtypeStruct((rows, width), jnp.float32),
+        in_specs=vmem(2),
+        out_specs=vmem(1)[0],
+        compiler_params=pltpu.CompilerParams(vmem_limit_bytes=32 * 2**20),
+    )(pieces, doc_emb)
 
 
 def solution(mesh):

time: 117 us -> 112 us (0.957)
  blocking collectives: 48.6 us -> 83.9 us
  waiting for transfers between devices: 25.7 us -> 0.01 us
  starting transfers between devices: 28.4 us -> 19.1 us
  Pallas kernels: 12.1 us -> 7.94 us
  other arithmetic: 1.56 us -> 0.22 us
    all_to_all x0 -> x1, blocking collectives: none -> 31.5 us  [body(): lax.all_to_all(part.reshape(PLANE_SIZE, rows, width), PLANE, split_axis=0...]
    all_to_all x1 -> x0, waiting for transfers between devices: 24.5 us -> none  [body(): lax.all_to_all(part.reshape(PLANE_SIZE, rows, width), PLANE, split_axis=0...]
    all_to_all x1 -> x0, starting transfers between devices: 5.79 us -> none  [body(): lax.all_to_all(part.reshape(PLANE_SIZE, rows, width), PLANE, split_axis=0...]
    pallas_call x2, Pallas kernels: 8.99 us -> 3.88 us  [push(): pl.pallas_call(functools.partial(push_kernel, side), out_shape=jax.ShapeD...]
    ppermute x1 -> x0, starting transfers between devices: 3.55 us -> none  [body(): neighbour = lax.ppermute(label_half, 'zb', [(0, 1), (1, 0)])]
    all_gather x0 -> x1, blocking collectives: none -> 3.5 us  [body(): pair = lax.all_gather(label_half, 'zb', axis=0, tiled=True)]
    ppermute x1 -> x0, waiting for transfers between devices: 1.2 us -> none  [body(): neighbour = lax.ppermute(label_half, 'zb', [(0, 1), (1, 0)])]
  transfers between devices with their start and end apart: 4 -> 2, of which waited for: 2 -> 0; matrix products, arithmetic and copies ran while one was open for 0% -> 0% of each run, Pallas kernels for 3% -> 3%
where the time goes in v4:
time: 112 us; the launch traced here: 111 us
  blocking collectives  83.9 us (75%)
  starting transfers between devices  19.1 us (17%)
  Pallas kernels  7.94 us (7%)
    all_gather x1, blocking collectives, body(): own_labels = lax.all_gather(pair, 'zp', axis=0, tiled=True)  48.9 us
    all_to_all x1, blocking collectives, body(): lax.all_to_all(part.reshape(PLANE_SIZE, rows, width), PLANE, split_axis=0...  31.5 us
    ppermute x1, starting transfers between devices, body(): other_labels = lax.ppermute(own_labels, 'c', [(0, 1), (1, 0)])  11.4 us
    all_to_all x1, starting transfers between devices, body(): lax.all_to_all(spread, PLANE, split_axis=0, concat_axis=0, tiled=True)  7.73 us
    pallas_call x2, Pallas kernels, push(): pl.pallas_call(functools.partial(push_kernel, side), out_shape=jax.ShapeD...  3.88 us
    all_gather x1, blocking collectives, body(): pair = lax.all_gather(label_half, 'zb', axis=0, tiled=True)  3.5 us
    pallas_call x1, Pallas kernels, body(): pl.pallas_call(prepare_kernel, out_shape=(jax.ShapeDtypeStruct(label_emb....  3.05 us
  transfers between devices with their start and end apart: 2, of which 0 were waited for; matrix products, arithmetic and copies ran while one was open for 0% of the time, Pallas kernels for 3%

profile of v4, /device:TPU:1, one launch (start us, length us, event | category | flops | bytes accessed | tf_op | source)
XLA Modules:
  0.0 111.3 jit_solution(235601360529703272)
XLA Ops:
  0.0 3.0 %shard_map.55 = (bf16[16,768]{1,0:T(8,128)(2,1)}, bf16[16,64,896]{2,1,0:T(8,128)(2,1)}) custom-call(bf16[64,768]{1,0:T(8,128)(2,1)} %doc_ref.3, bf16[16,768]{1,0:T(8,128)(2,1)} %label_ref.1, s32[8,1024]{1,0:T(8,128)} %bitcast.7), custom_call_target="tpu_custom_call" | custom-call | tf_op jit(solution)/shard_map/pallas_call | solution.py:144
  3.1 0.0 copy-start.2
  3.1 0.0 copy-start.3
  3.1 0.0 copy-start.1
  3.1 7.7 %all-to-all-start = ((bf16[16,64,896]{2,1,0:T(8,128)(2,1)}), bf16[16,64,896]{2,1,0:T(8,128)(2,1)S(1)}, u32[]{:S(2)}, u32[]{:S(2)}) async-start(bf16[16,64,896]{2,1,0:T(8,128)(2,1)} %get-tuple-element.7), calls=%async_computation | async-start | bytes 3670016 | tf_op jit(solution)/shard_map/all_to_all | solution.py:158
  10.8 0.0 copy-done.2
  10.8 3.5 %all_gather.6 = bf16[32,768]{1,0:T(8,128)(2,1)S(1)} all-gather(bf16[16,768]{1,0:T(8,128)(2,1)S(1)} %copy-done.2), channel_id=1, replica_groups=mesh['yh'=2,'zp'=16,'zb'=2,'x'=4,'yl'=2,'c'=2] {'zb'}, dimensions={0}, use_global_device_ids=true | all-gather | bytes 73728 | tf_op jit(solution)/shard_map/all_gather | solution.py:160
  14.3 48.9 %all_gather.7.labels_ref = bf16[512,768]{1,0:T(8,128)(2,1)S(1)} all-gather(bf16[32,768]{1,0:T(8,128)(2,1)S(1)} %all_gather.6), channel_id=1, replica_groups=mesh['yh'=2,'zp'=16,'zb'=2,'x'=4,'yl'=2,'c'=2] {'zp'}, dimensions={0}, use_global_device_ids=true | all-gather | bytes 835584 | tf_op jit(solution)/shard_map/all_gather | solution.py:161
  63.2 11.4 %collective-permute-start = (bf16[512,768]{1,0:T(8,128)(2,1)S(1)}, bf16[512,768]{1,0:T(8,128)(2,1)S(1)}, u32[]{:S(2)}, u32[]{:S(2)}) collective-permute-start(bf16[512,768]{1,0:T(8,128)(2,1)S(1)} %all_gather.7.labels_ref), channel_id=1, source_target_pairs={{0,1},{1,0},{2,3},{3,2},{4,5},{5,4},{6,7},{7,6},{8,9},{9,8},{10,11... | collective-permute-start | bytes 2359304 | tf_op jit(solution)/shard_map/ppermute | solution.py:162
  74.6 0.1 pad_add_fusion
  74.7 0.0 copy-done.3
  74.7 0.0 copy-done.1
  74.7 0.1 and_reduce_fusion
  74.8 0.0 all-to-all-done
  74.9 2.9 %shard_map.56.refs_0_ = f32[1024,768]{1,0:T(8,128)S(1)} custom-call(s32[8,256]{1,0:T(8,128)S(1)} %convert_element_type.3.live_ref, bf16[1024,896]{1,0:T(8,128)(2,1)S(1)} %bitcast.4, bf16[512,768]{1,0:T(8,128)(2,1)S(1)} %all_gather.7.labels_ref), custom_call_target="tpu_custom_call" | custom-call | flops 805306368 | bytes 6291456 | tf_op jit(solution)/shard_map/pallas_call | solution.py:174
  77.8 0.0 collective-permute-done.labels_ref
  77.8 1.0 shard_map.57
  78.8 0.0 copy-start
  78.8 31.5 %all_to_all.10.pieces_ref = bf16[16,64,768]{2,1,0:T(8,128)(2,1)S(1)} all-to-all(bf16[16,64,768]{2,1,0:T(8,128)(2,1)S(1)} %bitcast.6), channel_id=1, replica_groups=mesh['yh'=2,'zp'=16,'zb'=2,'x'=4,'yl'=2,'c'=2] {'yh','x','yl'}, dimensions={0} | all-to-all | bytes 3145728 | tf_op jit(solution)/shard_map/all_to_all | solution.py:190
  110.3 0.0 copy-done
  110.3 1.0 shard_map.58
  (3 shorter events, 0.0 us)
Async XLA Ops:
  3.1 7.8 %copy-start.2 = (bf16[16,768]{1,0:T(8,128)(2,1)S(1)}, bf16[16,768]{1,0:T(8,128)(2,1)}, u32[]{:S(2)}) copy-start(bf16[16,768]{1,0:T(8,128)(2,1)} %get-tuple-element.8) | copy-start | bytes 73732
  3.1 71.6 %copy-start.3 = (s32[256]{0:T(256)S(1)}, s32[256]{0:T(256)}, u32[]{:S(2)}) copy-start(s32[256]{0:T(256)} %param.8) | copy-start | bytes 3076
  3.1 71.6 %copy-start.1 = (s32[256,32]{0,1:T(8,128)S(1)}, s32[256,32]{0,1:T(8,128)}, u32[]{:S(2)}) copy-start(s32[256,32]{0,1:T(8,128)} %param.7) | copy-start | bytes 98308
  3.1 71.8 %all-to-all-start = ((bf16[16,64,896]{2,1,0:T(8,128)(2,1)}), bf16[16,64,896]{2,1,0:T(8,128)(2,1)S(1)}, u32[]{:S(2)}, u32[]{:S(2)}) async-start(bf16[16,64,896]{2,1,0:T(8,128)(2,1)} %get-tuple-element.7), calls=%async_computation | async-start | bytes 3670016 | tf_op jit(solution)/shard_map/all_to_all | solution.py:158
  63.2 14.6 %collective-permute-start = (bf16[512,768]{1,0:T(8,128)(2,1)S(1)}, bf16[512,768]{1,0:T(8,128)(2,1)S(1)}, u32[]{:S(2)}, u32[]{:S(2)}) collective-permute-start(bf16[512,768]{1,0:T(8,128)(2,1)S(1)} %all_gather.7.labels_ref), channel_id=1, source_target_pairs={{0,1},{1,0},{2,3},{3,2},{4,5},{5,4},{6,7},{7,6},{8,9},{9,8},{10,11... | collective-permute-start | bytes 2359304 | tf_op jit(solution)/shard_map/ppermute | solution.py:162
  78.8 31.5 %copy-start = (bf16[64,768]{1,0:T(8,128)(2,1)S(1)}, bf16[64,768]{1,0:T(8,128)(2,1)}, u32[]{:S(2)}) copy-start(bf16[64,768]{1,0:T(8,128)(2,1)} %doc_ref.3) | copy-start | bytes 294916

commit v5 on v4

--- a/solution.py
+++ b/solution.py
@@ -35,8 +35,7 @@
     return shard * 8 + yh * 4, (shard + 1 - 2 * core) * 8 + yh * 4
 
 
-def prepare_kernel(doc_ref, label_ref, pos_ref, half_ref, spread_ref, packed, sems):
-    half_ref[...] = unit_rows(label_ref[...])[0].astype(jnp.bfloat16)
+def prepare_kernel(doc_ref, pos_ref, spread_ref, packed, sems):
     rows, width = doc_ref.shape
     packed[:, :width] = unit_rows(doc_ref[...])[0].astype(jnp.bfloat16)
     _, _, _, x, yl, core = place()
@@ -61,13 +60,17 @@
 
 
 def push_kernel(side, live_ref, docs_ref, labels_ref, *refs):
-    before_ref, out_ref, tasks = refs if side else (None, *refs)
+    before_ref, out_ref, tasks, select = refs if side else (None, *refs)
     _, zp, zb, _, _, _ = place()
     width = labels_ref.shape[1]
     first = first_blocks()[side]
-    lane = lax.broadcasted_iota(jnp.int32, (1, 2 * LAB_BLK), 1)
-    upper = lane >= LAB_BLK
-    offset = lane % LAB_BLK
+    lane = lax.broadcasted_iota(jnp.int32, (1, LAB_BLK), 1)
+
+    row = lax.broadcasted_iota(jnp.int32, select.shape, 0)
+    group = lax.broadcasted_iota(jnp.int32, select.shape, 1) // 128
+    select[...] = jnp.where(
+        row == group, float(LAB_BLK), jnp.where(row == group + POS, 1.0, 0.0)
+    ).astype(jnp.bfloat16)
 
     number = jnp.int32(0)
     for run in range(RUNS):
@@ -90,7 +93,7 @@
             else:
                 out_ref[rows, :] = jnp.zeros((RUN, width), out_ref.dtype)
 
-    def work(task):
+    def coefficients(task):
         run, low, high, count = (tasks[4 * task + i] for i in range(4))
         rows = pl.ds(pl.multiple_of(run * RUN, RUN), RUN)
         panel = jnp.concatenate(
@@ -106,24 +109,30 @@
             (((1,), (1,)), ((), ())),
             preferred_element_type=jnp.float32,
         )
-        places = docs_ref[rows, width:].astype(jnp.float32)
-        pos_ids = places[:, :POS] * LAB_BLK + places[:, POS : 2 * POS]
-        ids = ((first + jnp.where(upper, high, low)) * LAB_BLK + offset).astype(jnp.float32)
-        hit = pos_ids[:, 0:1] == ids
-        for k in range(1, POS):
-            hit = hit | (pos_ids[:, k : k + 1] == ids)
-        coef = SCALE * (jax.nn.sigmoid(scores) - jnp.where(hit, 1.0, 0.0))
-        coef = jnp.where(upper & (count < 2), 0.0, coef).astype(jnp.bfloat16)
-        total = jnp.dot(coef, panel, preferred_element_type=jnp.float32)
-        if side:
-            total = total + before_ref[rows, :]
-        return rows, total.astype(out_ref.dtype)
-
-    @pl.loop(0, (number + 1) // 2)
-    def _(pair):
-        results = [work(2 * pair), work(jnp.minimum(2 * pair + 1, number - 1))]
-        for rows, total in results:
-            out_ref[rows, :] = total
+        pos_ids = jnp.dot(docs_ref[rows, width:], select[...], preferred_element_type=jnp.float32)
+        halves = []
+        for i, block in enumerate((low, high)):
+            ids = ((first + block) * LAB_BLK + lane).astype(jnp.float32)
+            hit = pos_ids[:, :128] == ids
+            for k in range(1, POS):
+                hit = hit | (pos_ids[:, k * 128 : (k + 1) * 128] == ids)
+            sigmoid = jax.nn.sigmoid(scores[:, i * LAB_BLK : (i + 1) * LAB_BLK])
+            coef = SCALE * (sigmoid - jnp.where(hit, 1.0, 0.0))
+            if i:
+                coef = jnp.where(count > 1, coef, 0.0)
+            halves.append(coef.astype(jnp.bfloat16))
+        return rows, jnp.concatenate(halves, axis=1), panel
+
+    @pl.loop(0, (number + 3) // 4)
+    def _(batch):
+        ready = [coefficients(jnp.minimum(4 * batch + i, number - 1)) for i in range(4)]
+        for rows, coef, panel in ready:
+            for start in range(0, width, 256):
+                columns = slice(start, start + 256)
+                total = jnp.dot(coef, panel[:, columns], preferred_element_type=jnp.float32)
+                if side:
+                    total = total + before_ref[rows, columns]
+                out_ref[rows, columns] = total.astype(out_ref.dtype)
 
 
 def finish_kernel(pieces_ref, doc_ref, out_ref):
@@ -141,23 +150,27 @@
 
 def body(doc_emb, label_emb, short_blocks, short_len, positives):
     rows, width = doc_emb.shape
-    label_half, spread = pl.pallas_call(
+    neighbour = lax.ppermute(label_emb, "zb", [(0, 1), (1, 0)])
+    spread = pl.pallas_call(
         prepare_kernel,
-        out_shape=(
-            jax.ShapeDtypeStruct(label_emb.shape, jnp.bfloat16),
-            jax.ShapeDtypeStruct((PLANE_SIZE, rows, width + 128), jnp.bfloat16),
-        ),
-        in_specs=vmem(3),
-        out_specs=(vmem(1)[0], pl.BlockSpec(memory_space=pl.ANY)),
+        out_shape=jax.ShapeDtypeStruct((PLANE_SIZE, rows, width + 128), jnp.bfloat16),
+        in_specs=vmem(2),
+        out_specs=pl.BlockSpec(memory_space=pl.ANY),
         scratch_shapes=[
             pltpu.VMEM((rows, width + 128), jnp.bfloat16),
             pltpu.SemaphoreType.DMA((PLANE_SIZE,)),
         ],
-    )(doc_emb, label_emb, positives.T)
-
+        cost_estimate=pl.CostEstimate(
+            flops=8 * rows * width, bytes_accessed=8 * 2**20, transcendentals=rows
+        ),
+    )(doc_emb, positives.T)
     docs = lax.all_to_all(spread, PLANE, split_axis=0, concat_axis=0, tiled=True)
     docs = docs.reshape(PLANE_SIZE * rows, width + 128)
-    pair = lax.all_gather(label_half, "zb", axis=0, tiled=True)
+    even = lax.axis_index("zb") == 0
+    pair = jnp.stack(
+        [jnp.where(even, label_emb, neighbour), jnp.where(even, neighbour, label_emb)]
+    ).reshape(2 * label_emb.shape[0], width)
+    pair = unit_rows(pair)[0].astype(jnp.bfloat16)
     own_labels = lax.all_gather(pair, "zp", axis=0, tiled=True)
     other_labels = lax.ppermute(own_labels, "c", [(0, 1), (1, 0)])
 
@@ -176,7 +189,10 @@
             out_shape=jax.ShapeDtypeStruct((RUNS * RUN, width), dtype),
             in_specs=[pl.BlockSpec(memory_space=pltpu.SMEM)] + vmem(len(operands)),
             out_specs=vmem(1)[0],
-            scratch_shapes=[pltpu.SMEM((4 * RUNS + 4,), jnp.int32)],
+            scratch_shapes=[
+                pltpu.SMEM((4 * RUNS + 4,), jnp.int32),
+                pltpu.VMEM((128, POS * 128), jnp.bfloat16),
+            ],
             compiler_params=pltpu.CompilerParams(vmem_limit_bytes=32 * 2**20),
             cost_estimate=pl.CostEstimate(
                 flops=4 * RUNS * RUN * 2 * LAB_BLK * width,

time: 112 us -> 106 us (0.946)
  blocking collectives: 83.9 us -> 75.2 us
  starting transfers between devices: 19.1 us -> 21 us
    ppermute x0 -> x1, starting transfers between devices: none -> 4.37 us  [body(): neighbour = lax.ppermute(label_emb, 'zb', [(0, 1), (1, 0)])]
    all_gather x1 -> x0, blocking collectives: 3.5 us -> none  [body(): pair = lax.all_gather(label_half, 'zb', axis=0, tiled=True)]
    all_to_all x1, blocking collectives: 31.5 us -> 28.9 us  [body(): lax.all_to_all(part.reshape(PLANE_SIZE, rows, width), PLANE, split_axis=0...]
    all_gather x1, blocking collectives: 48.9 us -> 46.3 us  [body(): own_labels = lax.all_gather(pair, 'zp', axis=0, tiled=True)]
    ppermute x1, starting transfers between devices: 11.4 us -> 9.69 us  [body(): other_labels = lax.ppermute(own_labels, 'c', [(0, 1), (1, 0)])]
  transfers between devices with their start and end apart: 2 -> 3, of which waited for: 0 -> 0; matrix products, arithmetic and copies ran while one was open for 0% -> 0% of each run, Pallas kernels for 3% -> 5%
where the time goes in v5:
time: 106 us; the launch traced here: 105 us
  blocking collectives  75.2 us (71%)
  starting transfers between devices  21 us (20%)
  Pallas kernels  8.35 us (8%)
    all_gather x1, blocking collectives, body(): own_labels = lax.all_gather(pair, 'zp', axis=0, tiled=True)  46.3 us
    all_to_all x1, blocking collectives, body(): lax.all_to_all(part.reshape(PLANE_SIZE, rows, width), PLANE, split_axis=0...  28.9 us
    ppermute x1, starting transfers between devices, body(): other_labels = lax.ppermute(own_labels, 'c', [(0, 1), (1, 0)])  9.69 us
    all_to_all x1, starting transfers between devices, body(): lax.all_to_all(spread, PLANE, split_axis=0, concat_axis=0, tiled=True)  6.9 us
    pallas_call x2, Pallas kernels, push(): pl.pallas_call(functools.partial(push_kernel, side), out_shape=jax.ShapeD...  4.91 us
    ppermute x1, starting transfers between devices, body(): neighbour = lax.ppermute(label_emb, 'zb', [(0, 1), (1, 0)])  4.37 us
    pallas_call x1, Pallas kernels, body(): pl.pallas_call(prepare_kernel, out_shape=jax.ShapeDtypeStruct((PLANE_SIZE...  2.43 us
  transfers between devices with their start and end apart: 3, of which 0 were waited for; matrix products, arithmetic and copies ran while one was open for 0% of the time, Pallas kernels for 5%

profile of v5, /device:TPU:1, one launch (start us, length us, event | category | flops | bytes accessed | tf_op | source)
XLA Modules:
  0.0 105.2 jit_solution(4092944190708421116)
XLA Ops:
  0.0 4.4 %collective-permute-start = (bf16[16,768]{1,0:T(8,128)(2,1)}, bf16[16,768]{1,0:T(8,128)(2,1)S(1)}, u32[]{:S(2)}, u32[]{:S(2)}) collective-permute-start(bf16[16,768]{1,0:T(8,128)(2,1)} %param.6), channel_id=1, source_target_pairs={{0,16},{16,0},{1,17},{17,1},{2,18},{18,2},{3,19},{19,3},{4,20},{20... | collective-permute-start | bytes 73736 | tf_op jit(solution)/shard_map/ppermute | solution.py:153
  4.4 2.4 %shard_map.55 = bf16[16,64,896]{2,1,0:T(8,128)(2,1)} custom-call(bf16[64,768]{1,0:T(8,128)(2,1)} %doc_ref.3, s32[8,1024]{1,0:T(8,128)} %bitcast.15), custom_call_target="tpu_custom_call" | custom-call | flops 393216 | bytes 8388608 | tf_op jit(solution)/shard_map/pallas_call | solution.py:154
  6.8 0.0 copy-start.2
  6.8 0.0 copy-start.3
  6.8 0.0 copy-start.1
  6.9 6.9 %all-to-all-start = ((bf16[16,64,896]{2,1,0:T(8,128)(2,1)}), bf16[16,64,896]{2,1,0:T(8,128)(2,1)S(1)}, u32[]{:S(2)}, u32[]{:S(2)}) async-start(bf16[16,64,896]{2,1,0:T(8,128)(2,1)} %shard_map.55), calls=%async_computation | async-start | bytes 3670016 | tf_op jit(solution)/shard_map/all_to_all | solution.py:167
  13.8 0.0 collective-permute-done
  13.8 0.0 copy-done.2
  13.8 0.1 multiply_reduce_fusion
  13.9 0.1 sqrt.12
  14.0 0.1 fusion
  14.1 46.3 %all_gather.3.labels_ref = bf16[512,768]{1,0:T(8,128)(2,1)S(1)} all-gather(bf16[32,768]{1,0:T(8,128)(2,1)S(1)} %fusion), channel_id=1, replica_groups=mesh['yh'=2,'zp'=16,'zb'=2,'x'=4,'yl'=2,'c'=2] {'zp'}, dimensions={0}, use_global_device_ids=true | all-gather | bytes 835584 | tf_op jit(solution)/shard_map/all_gather | solution.py:174
  60.4 9.7 %collective-permute-start.1 = (bf16[512,768]{1,0:T(8,128)(2,1)S(1)}, bf16[512,768]{1,0:T(8,128)(2,1)S(1)}, u32[]{:S(2)}, u32[]{:S(2)}) collective-permute-start(bf16[512,768]{1,0:T(8,128)(2,1)S(1)} %all_gather.3.labels_ref), channel_id=1, source_target_pairs={{0,1},{1,0},{2,3},{3,2},{4,5},{5,4},{6,7},{7,6},{8,9},{9,8},{10,11... | collective-permute-start | bytes 2359304 | tf_op jit(solution)/shard_map/ppermute | solution.py:175
  70.1 0.1 pad_add_fusion
  70.2 0.0 copy-done.3
  70.2 0.0 copy-done.1
  70.2 0.1 and_reduce_fusion
  70.4 0.0 all-to-all-done
  70.4 3.0 %shard_map.56.refs_0_ = f32[1024,768]{1,0:T(8,128)S(1)} custom-call(s32[8,256]{1,0:T(8,128)S(1)} %convert_element_type.15.live_ref, bf16[1024,896]{1,0:T(8,128)(2,1)S(1)} %bitcast.12, bf16[512,768]{1,0:T(8,128)(2,1)S(1)} %all_gather.3.labels_ref), custom_call_target="tpu_custom_call" | custom-call | flops 805306368 | bytes 6291456 | tf_op jit(solution)/shard_map/pallas_call | solution.py:187
  73.4 0.0 collective-permute-done.1.labels_ref
  73.4 1.9 %shard_map.57 = bf16[1024,768]{1,0:T(8,128)(2,1)S(1)} custom-call(s32[8,256]{1,0:T(8,128)S(1)} %convert_element_type.15.live_ref, bf16[1024,896]{1,0:T(8,128)(2,1)S(1)} %bitcast.13, bf16[512,768]{1,0:T(8,128)(2,1)S(1)} %collective-permute-done.1.labels_ref, f32[1024,768]{1,0:T(8,128)S(1)} %shard_map.56.refs_0_), custom_call_target="tpu_custom_call" | custom-call | flops 805306368 | bytes 6291456 | tf_op jit(solution)/shard_map/pallas_call | solution.py:187
  75.3 0.0 copy-start
  75.3 28.9 %all_to_all.10.pieces_ref = bf16[16,64,768]{2,1,0:T(8,128)(2,1)S(1)} all-to-all(bf16[16,64,768]{2,1,0:T(8,128)(2,1)S(1)} %bitcast.14), channel_id=1, replica_groups=mesh['yh'=2,'zp'=16,'zb'=2,'x'=4,'yl'=2,'c'=2] {'yh','x','yl'}, dimensions={0} | all-to-all | bytes 3145728 | tf_op jit(solution)/shard_map/all_to_all | solution.py:206
  104.2 0.0 copy-done
  104.2 1.0 shard_map.58
  (6 shorter events, 0.1 us)
Async XLA Ops:
  0.0 13.8 %collective-permute-start = (bf16[16,768]{1,0:T(8,128)(2,1)}, bf16[16,768]{1,0:T(8,128)(2,1)S(1)}, u32[]{:S(2)}, u32[]{:S(2)}) collective-permute-start(bf16[16,768]{1,0:T(8,128)(2,1)} %param.6), channel_id=1, source_target_pairs={{0,16},{16,0},{1,17},{17,1},{2,18},{18,2},{3,19},{19,3},{4,20},{20... | collective-permute-start | bytes 73736 | tf_op jit(solution)/shard_map/ppermute | solution.py:153
  6.8 7.0 %copy-start.2 = (bf16[16,768]{1,0:T(8,128)(2,1)S(1)}, bf16[16,768]{1,0:T(8,128)(2,1)}, u32[]{:S(2)}) copy-start(bf16[16,768]{1,0:T(8,128)(2,1)} %param.6) | copy-start | bytes 73732
  6.8 63.4 %copy-start.3 = (s32[256]{0:T(256)S(1)}, s32[256]{0:T(256)}, u32[]{:S(2)}) copy-start(s32[256]{0:T(256)} %param.8) | copy-start | bytes 3076
  6.8 63.4 %copy-start.1 = (s32[256,32]{0,1:T(8,128)S(1)}, s32[256,32]{0,1:T(8,128)}, u32[]{:S(2)}) copy-start(s32[256,32]{0,1:T(8,128)} %param.7) | copy-start | bytes 98308
  6.9 63.5 %all-to-all-start = ((bf16[16,64,896]{2,1,0:T(8,128)(2,1)}), bf16[16,64,896]{2,1,0:T(8,128)(2,1)S(1)}, u32[]{:S(2)}, u32[]{:S(2)}) async-start(bf16[16,64,896]{2,1,0:T(8,128)(2,1)} %shard_map.55), calls=%async_computation | async-start | bytes 3670016 | tf_op jit(solution)/shard_map/all_to_all | solution.py:167
  60.4 12.9 %collective-permute-start.1 = (bf16[512,768]{1,0:T(8,128)(2,1)S(1)}, bf16[512,768]{1,0:T(8,128)(2,1)S(1)}, u32[]{:S(2)}, u32[]{:S(2)}) collective-permute-start(bf16[512,768]{1,0:T(8,128)(2,1)S(1)} %all_gather.3.labels_ref), channel_id=1, source_target_pairs={{0,1},{1,0},{2,3},{3,2},{4,5},{5,4},{6,7},{7,6},{8,9},{9,8},{10,11... | collective-permute-start | bytes 2359304 | tf_op jit(solution)/shard_map/ppermute | solution.py:175
  75.3 28.9 %copy-start = (bf16[64,768]{1,0:T(8,128)(2,1)S(1)}, bf16[64,768]{1,0:T(8,128)(2,1)}, u32[]{:S(2)}) copy-start(bf16[64,768]{1,0:T(8,128)(2,1)} %doc_ref.3) | copy-start | bytes 294916

commit v6 on v5

--- a/solution.py
+++ b/solution.py
@@ -1,5 +1,3 @@
-import functools
-
 import jax
 import jax.numpy as jnp
 from jax import lax
@@ -29,16 +27,16 @@
     return tuple(lax.axis_index(a) for a in AXES)
 
 
-def first_blocks():
-    yh, _, _, x, yl, core = place()
-    shard = (x * 2 + yl) * 2 + core
-    return shard * 8 + yh * 4, (shard + 1 - 2 * core) * 8 + yh * 4
-
-
-def prepare_kernel(doc_ref, pos_ref, spread_ref, packed, sems):
+def first_block(side):
+    yh, _, _, x, yl, _ = place()
+    return ((x * 2 + yl) * 2 + side) * 8 + yh * 4
+
+
+def prepare_kernel(doc_ref, other_ref, pos_ref, spread_ref, packed, sems):
     rows, width = doc_ref.shape
-    packed[:, :width] = unit_rows(doc_ref[...])[0].astype(jnp.bfloat16)
-    _, _, _, x, yl, core = place()
+    packed[:rows, :width] = unit_rows(doc_ref[...])[0].astype(jnp.bfloat16)
+    packed[rows:, :width] = unit_rows(other_ref[...])[0].astype(jnp.bfloat16)
+    _, _, _, x, yl, _ = place()
     ids = pos_ref[:, pl.ds(pl.multiple_of((x * 2 + yl) * 128, 128), 128)]
     parts = jnp.concatenate(
         [
@@ -48,8 +46,7 @@
         ],
         axis=0,
     )
-    parts = parts.T
-    packed[:, width:] = jnp.where(core == 0, parts[:rows], parts[rows:]).astype(jnp.bfloat16)
+    packed[:, width:] = parts.T.astype(jnp.bfloat16)
     copies = [
         pltpu.make_async_copy(packed, spread_ref.at[i], sems.at[i]) for i in range(PLANE_SIZE)
     ]
@@ -59,11 +56,20 @@
         copy.wait()
 
 
-def push_kernel(side, live_ref, docs_ref, labels_ref, *refs):
-    before_ref, out_ref, tasks, select = refs if side else (None, *refs)
+def push_kernel(live_ref, kept_ref, sent_ref, got_ref, out_ref, tasks, select, total):
+    core = place()[-1]
+    for mine, docs_ref, labels_ref in ((0, kept_ref, got_ref), (1, got_ref, sent_ref)):
+
+        @pl.when(core == mine)
+        def _():
+            push_side(0, live_ref, docs_ref, labels_ref, None, total, tasks, select)
+            push_side(1, live_ref, docs_ref, labels_ref, total, out_ref, tasks, select)
+
+
+def push_side(side, live_ref, docs_ref, labels_ref, before_ref, out_ref, tasks, select):
     _, zp, zb, _, _, _ = place()
-    width = labels_ref.shape[1]
-    first = first_blocks()[side]
+    width = out_ref.shape[1]
+    first = first_block(side)
     lane = lax.broadcasted_iota(jnp.int32, (1, LAB_BLK), 1)
 
     row = lax.broadcasted_iota(jnp.int32, select.shape, 0)
@@ -98,7 +104,7 @@
         rows = pl.ds(pl.multiple_of(run * RUN, RUN), RUN)
         panel = jnp.concatenate(
             [
-                labels_ref[pl.ds(pl.multiple_of(b * LAB_BLK, LAB_BLK), LAB_BLK), :]
+                labels_ref[pl.ds(pl.multiple_of((4 * side + b) * LAB_BLK, LAB_BLK), LAB_BLK), :width]
                 for b in (low, high)
             ],
             axis=0,
@@ -150,32 +156,41 @@
 
 def body(doc_emb, label_emb, short_blocks, short_len, positives):
     rows, width = doc_emb.shape
-    neighbour = lax.ppermute(label_emb, "zb", [(0, 1), (1, 0)])
-    spread = pl.pallas_call(
-        prepare_kernel,
-        out_shape=jax.ShapeDtypeStruct((PLANE_SIZE, rows, width + 128), jnp.bfloat16),
-        in_specs=vmem(2),
-        out_specs=pl.BlockSpec(memory_space=pl.ANY),
-        scratch_shapes=[
-            pltpu.VMEM((rows, width + 128), jnp.bfloat16),
-            pltpu.SemaphoreType.DMA((PLANE_SIZE,)),
-        ],
-        cost_estimate=pl.CostEstimate(
-            flops=8 * rows * width, bytes_accessed=8 * 2**20, transcendentals=rows
-        ),
-    )(doc_emb, positives.T)
-    docs = lax.all_to_all(spread, PLANE, split_axis=0, concat_axis=0, tiled=True)
-    docs = docs.reshape(PLANE_SIZE * rows, width + 128)
-    even = lax.axis_index("zb") == 0
-    pair = jnp.stack(
-        [jnp.where(even, label_emb, neighbour), jnp.where(even, neighbour, label_emb)]
-    ).reshape(2 * label_emb.shape[0], width)
-    pair = unit_rows(pair)[0].astype(jnp.bfloat16)
-    own_labels = lax.all_gather(pair, "zp", axis=0, tiled=True)
-    other_labels = lax.ppermute(own_labels, "c", [(0, 1), (1, 0)])
+    other_docs = lax.ppermute(doc_emb, "c", [(0, 1), (1, 0)])
+    near_labels = lax.all_gather(label_emb, ("zb", "c"), axis=0, tiled=True)
+
+    def gather_labels(operands):
+        half = unit_rows(operands[2])[0].astype(jnp.bfloat16)
+        labels = lax.all_gather(half.astype(jnp.float16), "zp", axis=0, tiled=True)
+        labels = labels.reshape(16, 2, 2, label_emb.shape[0], width).transpose(2, 0, 1, 3, 4)
+        labels = labels.reshape(-1, width).astype(jnp.bfloat16)
+        labels = jnp.pad(labels, ((0, 0), (0, 128)))
+        return jnp.zeros_like(labels), labels
+
+    def gather_docs(operands):
+        spread = pl.pallas_call(
+            prepare_kernel,
+            out_shape=jax.ShapeDtypeStruct((PLANE_SIZE, 2 * rows, width + 128), jnp.bfloat16),
+            in_specs=vmem(3),
+            out_specs=pl.BlockSpec(memory_space=pl.ANY),
+            scratch_shapes=[
+                pltpu.VMEM((2 * rows, width + 128), jnp.bfloat16),
+                pltpu.SemaphoreType.DMA((PLANE_SIZE,)),
+            ],
+        )(operands[0], operands[1], operands[3])
+        docs = lax.all_to_all(spread, PLANE, split_axis=0, concat_axis=0, tiled=True)
+        return tuple(docs[:, i * rows : (i + 1) * rows].reshape(-1, width + 128) for i in range(2))
+
+    kept, sent = lax.cond(
+        lax.axis_index("c") == 1,
+        gather_labels,
+        gather_docs,
+        (doc_emb, other_docs, near_labels, positives.T),
+    )
+    got = lax.ppermute(sent, "c", [(0, 1), (1, 0)])
 
     grid = jnp.arange(4, dtype=jnp.int32)
-    block_ids = jnp.concatenate([first + grid for first in first_blocks()])
+    block_ids = jnp.concatenate([first_block(side) + grid for side in range(2)])
     slot = jnp.arange(short_blocks.shape[1], dtype=jnp.int32)
     live = jnp.any(
         (short_blocks.T[None] == block_ids[:, None, None])
@@ -183,26 +198,18 @@
         axis=1,
     ).astype(jnp.int32)
 
-    def push(side, dtype, *operands):
-        return pl.pallas_call(
-            functools.partial(push_kernel, side),
-            out_shape=jax.ShapeDtypeStruct((RUNS * RUN, width), dtype),
-            in_specs=[pl.BlockSpec(memory_space=pltpu.SMEM)] + vmem(len(operands)),
-            out_specs=vmem(1)[0],
-            scratch_shapes=[
-                pltpu.SMEM((4 * RUNS + 4,), jnp.int32),
-                pltpu.VMEM((128, POS * 128), jnp.bfloat16),
-            ],
-            compiler_params=pltpu.CompilerParams(vmem_limit_bytes=32 * 2**20),
-            cost_estimate=pl.CostEstimate(
-                flops=4 * RUNS * RUN * 2 * LAB_BLK * width,
-                bytes_accessed=6 * 2**20,
-                transcendentals=2 * RUNS * RUN * 2 * LAB_BLK,
-            ),
-        )(live, *operands)
-
-    part = push(0, jnp.float32, docs, own_labels)
-    part = push(1, jnp.bfloat16, docs, other_labels, part)
+    part = pl.pallas_call(
+        push_kernel,
+        out_shape=jax.ShapeDtypeStruct((RUNS * RUN, width), jnp.bfloat16),
+        in_specs=[pl.BlockSpec(memory_space=pltpu.SMEM)] + vmem(3),
+        out_specs=vmem(1)[0],
+        scratch_shapes=[
+            pltpu.SMEM((4 * RUNS + 4,), jnp.int32),
+            pltpu.VMEM((128, POS * 128), jnp.bfloat16),
+            pltpu.VMEM((RUNS * RUN, width), jnp.float32),
+        ],
+        compiler_params=pltpu.CompilerParams(vmem_limit_bytes=32 * 2**20),
+    )(live, kept, sent, got)
     pieces = lax.all_to_all(
         part.reshape(PLANE_SIZE, rows, width), PLANE, split_axis=0, concat_axis=0, tiled=True
     )

time: 106 us -> 108 us (1.019)
  waiting for transfers between devices: 0.01 us -> 3.7 us
  starting transfers between devices: 21 us -> 18 us
  local copies, waits for them, and re-layouts: 0.11 us -> 2.97 us
  Pallas kernels: 8.35 us -> 5.68 us
  blocking collectives: 75.2 us -> 76.9 us
    all_to_all x1 -> x0, starting transfers between devices: 6.9 us -> none  [body(): lax.all_to_all(spread, PLANE, split_axis=0, concat_axis=0, tiled=True)]
    ppermute x2, starting transfers between devices: 14.1 us -> 18 us  [the longest x1 16.1 us: body(): other_docs = lax.ppermute(doc_emb, 'c', [(0, 1), (1, 0)])]
    ppermute x2, waiting for transfers between devices: 0.01 us -> 3.7 us  [the longest x1 3.7 us: body(): got = lax.ppermute(sent, 'c', [(0, 1), (1, 0)])]
    pallas_call x3 -> x1, Pallas kernels: 7.34 us -> 4.67 us  [body(): pl.pallas_call(push_kernel, out_shape=jax.ShapeDtypeStruct((RUNS * RUN, w...]
    pad x0 -> x1, local copies, waits for them, and re-layouts: none -> 1.36 us  [gather_labels(): labels = jnp.pad(labels, ((0, 0), (0, 128)))]
    all_gather x1 -> x2, blocking collectives: 46.3 us -> 47.7 us  [the longest x1 42.3 us: gather_labels(): labels = lax.all_gather(half.astype(jnp.float16), 'zp', axis=0, tiled=True)]
    unnamed x8, local copies, waits for them, and re-layouts: 0.03 us -> 1.26 us
  transfers between devices with their start and end apart: 3 -> 2, of which waited for: 0 -> 1; matrix products, arithmetic and copies ran while one was open for 0% -> 0% of each run, Pallas kernels for 5% -> 0%
where the time goes in v6:
time: 108 us
  blocking collectives  76.9 us (71%)
  starting transfers between devices  18 us (17%)
  Pallas kernels  5.68 us (5%)
  waiting for transfers between devices  3.7 us (3%)
  local copies, waits for them, and re-layouts  2.97 us (3%)
    all_gather x1, blocking collectives, gather_labels(): labels = lax.all_gather(half.astype(jnp.float16), 'zp', axis=0, tiled=True)  42.3 us
    all_to_all x1, blocking collectives, body(): lax.all_to_all(part.reshape(PLANE_SIZE, rows, width), PLANE, split_axis=0...  29.3 us
    ppermute x1, starting transfers between devices, body(): other_docs = lax.ppermute(doc_emb, 'c', [(0, 1), (1, 0)])  16.1 us
    all_gather x1, blocking collectives, body(): near_labels = lax.all_gather(label_emb, ('zb', 'c'), axis=0, tiled=True)  5.39 us
    pallas_call x1, Pallas kernels, body(): pl.pallas_call(push_kernel, out_shape=jax.ShapeDtypeStruct((RUNS * RUN, w...  4.67 us
    ppermute x1, waiting for transfers between devices, body(): got = lax.ppermute(sent, 'c', [(0, 1), (1, 0)])  3.7 us
  transfers between devices with their start and end apart: 2, of which 1 were waited for; matrix products, arithmetic and copies ran while one was open for 0% of the time, Pallas kernels for 0%

profile of v6, /device:TPU:1, one launch (start us, length us, event | category | flops | bytes accessed | tf_op | source)
XLA Modules:
  0.0 108.1 jit_solution(9213545017095483318)
XLA Ops:
  0.0 16.1 %collective-permute-start = (bf16[64,768]{1,0:T(8,128)(2,1)}, bf16[64,768]{1,0:T(8,128)(2,1)S(1)}, u32[]{:S(2)}, u32[]{:S(2)}) collective-permute-start(bf16[64,768]{1,0:T(8,128)(2,1)} %doc_ref.1), channel_id=1, source_target_pairs={{0,1},{1,0},{2,3},{3,2},{4,5},{5,4},{6,7},{7,6},{8,9},{9,8},{10,11... | collective-permute-start | bytes 294920 | tf_op jit(solution)/shard_map/ppermute | solution.py:159
  16.1 5.4 %all_gather.9 = bf16[64,768]{1,0:T(8,128)(2,1)S(1)} all-gather(bf16[16,768]{1,0:T(8,128)(2,1)} %param.8), channel_id=1, replica_groups=mesh['yh'=2,'zp'=16,'zb'=2,'x'=4,'yl'=2,'c'=2] {'zb','c'}, dimensions={0}, use_global_device_ids=true | all-gather | bytes 122880 | tf_op jit(solution)/shard_map/all_gather | solution.py:160
  21.5 0.0 collective-permute-done
  21.5 0.0 copy-start.3
  21.5 0.0 copy-start.2
  21.5 44.5 %conditional.1 = (bf16[1024,896]{1,0:T(8,128)(2,1)S(1)}, bf16[1024,896]{1,0:T(8,128)(2,1)}) conditional(s32[]{:T(128)} %convert_element_type.30, (bf16[64,768]{1,0:T(8,128)(2,1)}, bf16[64,768]{1,0:T(8,128)(2,1)S(1)}, s32[8,1024]{1,0:T(8,128)}) %tuple.18, bf16[64,768]{1,0:T(8,128)(2,1)S(1)} %all_gather.9), branch_computations={%region_1.2_spmd, %region_2.4_spmd} | conditional | flops 1130496 | bytes 14680080 | solution.py:184
  21.5 0.1 fusion
  21.6 0.1 fusion.2
  21.7 42.3 %all-gather.1 = f16[1024,768]{1,0:T(8,128)(2,1)S(1)} all-gather(f16[64,768]{1,0:T(8,128)(2,1)S(1)} %fusion.2), channel_id=1, replica_groups=mesh['yh'=2,'zp'=16,'zb'=2,'x'=4,'yl'=2,'c'=2] {'zp'}, dimensions={0}, use_global_device_ids=true | all-gather | bytes 1671168 | tf_op jit(solution)/shard_map/cond/branch_1_fun/all_gather | solution.py:164
  64.0 0.2 convert_element_type.23
  64.3 0.2 copy.7
  64.5 1.4 %pad.3 = bf16[1024,896]{1,0:T(8,128)(2,1)} pad(bf16[1024,768]{1,0:T(8,128)(2,1)S(1)} %bitcast.12, bf16[]{:T(256)} %constant.9.clone), padding=0_0x0_128 | pad | bytes 3407874 | tf_op jit(solution)/shard_map/cond/branch_1_fun/jit(_pad)/pad | solution.py:167
  65.8 0.1 broadcast.25
  66.0 0.0 copy-start
  66.0 1.2 %copy-done = bf16[1024,896]{1,0:T(8,128)(2,1)} copy-done((bf16[1024,896]{1,0:T(8,128)(2,1)}, bf16[1024,896]{1,0:T(8,128)(2,1)S(1)}, u32[]{:S(2)}) %copy-start) | copy-done | bytes 1835032
  67.2 1.9 %collective-permute-start.1 = (bf16[1024,896]{1,0:T(8,128)(2,1)}, bf16[1024,896]{1,0:T(8,128)(2,1)S(1)}, u32[]{:S(2)}, u32[]{:S(2)}) collective-permute-start(bf16[1024,896]{1,0:T(8,128)(2,1)} %get-tuple-element.18.sent_ref), channel_id=1, source_target_pairs={{0,1},{1,0},{2,3},{3,2},{4,5},{5,4},{6,7},{7,6},{8,9},{9,8},{10,11... | collective-permute-start | bytes 5505032 | tf_op jit(solution)/shard_map/ppermute | solution.py:190
  69.2 0.1 pad_add_fusion
  69.2 0.0 copy-done.3
  69.3 0.0 copy-done.2
  69.3 0.1 and_reduce_fusion
  69.4 3.7 %collective-permute-done.1.got_ref = bf16[1024,896]{1,0:T(8,128)(2,1)S(1)} collective-permute-done((bf16[1024,896]{1,0:T(8,128)(2,1)}, bf16[1024,896]{1,0:T(8,128)(2,1)S(1)}, u32[]{:S(2)}, u32[]{:S(2)}) %collective-permute-start.1) | collective-permute-done | bytes 1835040 | tf_op jit(solution)/shard_map/ppermute | solution.py:190
  73.1 4.7 %shard_map.55 = bf16[1024,768]{1,0:T(8,128)(2,1)S(1)} custom-call(s32[8,256]{1,0:T(8,128)S(1)} %convert_element_type.29.live_ref, bf16[1024,896]{1,0:T(8,128)(2,1)} %copy-done, bf16[1024,896]{1,0:T(8,128)(2,1)} %get-tuple-element.18.sent_ref, bf16[1024,896]{1,0:T(8,128)(2,1)S(1)} %collective-permute-done.1.got_ref), custom_call_target="tpu_custom_call" | custom-call | tf_op jit(solution)/shard_map/pallas_call | solution.py:201
  77.8 0.0 copy-start.1
  77.8 29.3 %all_to_all.10.pieces_ref = bf16[16,64,768]{2,1,0:T(8,128)(2,1)S(1)} all-to-all(bf16[16,64,768]{2,1,0:T(8,128)(2,1)S(1)} %bitcast.9), channel_id=1, replica_groups=mesh['yh'=2,'zp'=16,'zb'=2,'x'=4,'yl'=2,'c'=2] {'yh','x','yl'}, dimensions={0} | all-to-all | bytes 3145728 | tf_op jit(solution)/shard_map/all_to_all | solution.py:213
  107.1 0.0 copy-done.1
  107.1 1.0 shard_map.56
  (4 shorter events, 0.0 us)
Async XLA Ops:
  0.0 21.5 %collective-permute-start = (bf16[64,768]{1,0:T(8,128)(2,1)}, bf16[64,768]{1,0:T(8,128)(2,1)S(1)}, u32[]{:S(2)}, u32[]{:S(2)}) collective-permute-start(bf16[64,768]{1,0:T(8,128)(2,1)} %doc_ref.1), channel_id=1, source_target_pairs={{0,1},{1,0},{2,3},{3,2},{4,5},{5,4},{6,7},{7,6},{8,9},{9,8},{10,11... | collective-permute-start | bytes 294920 | tf_op jit(solution)/shard_map/ppermute | solution.py:159
  21.5 47.8 %copy-start.3 = (s32[256]{0:T(256)S(1)}, s32[256]{0:T(256)}, u32[]{:S(2)}) copy-start(s32[256]{0:T(256)} %param.10) | copy-start | bytes 3076
  21.5 47.8 %copy-start.2 = (s32[256,32]{0,1:T(8,128)S(1)}, s32[256,32]{0,1:T(8,128)}, u32[]{:S(2)}) copy-start(s32[256,32]{0,1:T(8,128)} %param.9) | copy-start | bytes 98308
  66.0 1.3 %copy-start = (bf16[1024,896]{1,0:T(8,128)(2,1)}, bf16[1024,896]{1,0:T(8,128)(2,1)S(1)}, u32[]{:S(2)}) copy-start(bf16[1024,896]{1,0:T(8,128)(2,1)S(1)} %get-tuple-element.17.kept_ref) | copy-start | bytes 5505028
  67.2 5.9 %collective-permute-start.1 = (bf16[1024,896]{1,0:T(8,128)(2,1)}, bf16[1024,896]{1,0:T(8,128)(2,1)S(1)}, u32[]{:S(2)}, u32[]{:S(2)}) collective-permute-start(bf16[1024,896]{1,0:T(8,128)(2,1)} %get-tuple-element.18.sent_ref), channel_id=1, source_target_pairs={{0,1},{1,0},{2,3},{3,2},{4,5},{5,4},{6,7},{7,6},{8,9},{9,8},{10,11... | collective-permute-start | bytes 5505032 | tf_op jit(solution)/shard_map/ppermute | solution.py:190
  77.8 29.3 %copy-start.1 = (bf16[64,768]{1,0:T(8,128)(2,1)S(1)}, bf16[64,768]{1,0:T(8,128)(2,1)}, u32[]{:S(2)}) copy-start(bf16[64,768]{1,0:T(8,128)(2,1)} %doc_ref.1) | copy-start | bytes 294916

commit v7 on v5

--- a/solution.py
+++ b/solution.py
@@ -72,29 +72,33 @@
         row == group, float(LAB_BLK), jnp.where(row == group + POS, 1.0, 0.0)
     ).astype(jnp.bfloat16)
 
+    def listed(which, run):
+        column = (run // 4) * 128 + (zp * 2 + zb) * 4 + run % 4
+        live = [live_ref[which * 4 + i, column] for i in range(4)]
+        low = jnp.where(live[0] > 0, 0, jnp.where(live[1] > 0, 1, jnp.where(live[2] > 0, 2, 3)))
+        high = jnp.where(live[3] > 0, 3, jnp.where(live[2] > 0, 2, jnp.where(live[1] > 0, 1, 0)))
+        return live[0] + live[1] + live[2] + live[3], low, high
+
     number = jnp.int32(0)
     for run in range(RUNS):
-        column = (run // 4) * 128 + (zp * 2 + zb) * 4 + run % 4
-        live = [live_ref[side * 4 + i, column] for i in range(4)]
-        count = live[0] + live[1] + live[2] + live[3]
-        low = jnp.where(live[0] > 0, 0, jnp.where(live[1] > 0, 1, jnp.where(live[2] > 0, 2, 3)))
-        high = jnp.where(live[3] > 0, 3, jnp.where(live[2] > 0, 2, jnp.where(live[1] > 0, 1, 0)))
-        tasks[4 * number] = run
-        tasks[4 * number + 1] = low
-        tasks[4 * number + 2] = high
-        tasks[4 * number + 3] = count
+        count, low, high = listed(side, run)
+        begun = listed(0, run)[0] if side else jnp.int32(0)
+        for i, value in enumerate((run, low, high, count, begun)):
+            tasks[5 * number + i] = value
         number = number + jnp.where(count > 0, 1, 0)
-
-        @pl.when(count == 0)
-        def _():
+        if side:
             rows = pl.ds(run * RUN, RUN)
-            if side:
+
+            @pl.when((count == 0) & (begun > 0))
+            def _():
                 out_ref[rows, :] = before_ref[rows, :].astype(out_ref.dtype)
-            else:
+
+            @pl.when((count == 0) & (begun == 0))
+            def _():
                 out_ref[rows, :] = jnp.zeros((RUN, width), out_ref.dtype)
 
     def coefficients(task):
-        run, low, high, count = (tasks[4 * task + i] for i in range(4))
+        run, low, high, count, begun = (tasks[5 * task + i] for i in range(5))
         rows = pl.ds(pl.multiple_of(run * RUN, RUN), RUN)
         panel = jnp.concatenate(
             [
@@ -121,18 +125,27 @@
             if i:
                 coef = jnp.where(count > 1, coef, 0.0)
             halves.append(coef.astype(jnp.bfloat16))
-        return rows, jnp.concatenate(halves, axis=1), panel
-
-    @pl.loop(0, (number + 3) // 4)
-    def _(batch):
-        ready = [coefficients(jnp.minimum(4 * batch + i, number - 1)) for i in range(4)]
-        for rows, coef, panel in ready:
-            for start in range(0, width, 256):
-                columns = slice(start, start + 256)
+        return rows, jnp.concatenate(halves, axis=1), panel, begun
+
+    def batch(start, size):
+        ready = [coefficients(jnp.minimum(start + i, number - 1)) for i in range(size)]
+        for rows, coef, panel, begun in ready:
+            for left in range(0, width, 256):
+                columns = slice(left, left + 256)
                 total = jnp.dot(coef, panel[:, columns], preferred_element_type=jnp.float32)
                 if side:
-                    total = total + before_ref[rows, columns]
+                    total = jnp.where(begun > 0, total + before_ref[rows, columns], total)
                 out_ref[rows, columns] = total.astype(out_ref.dtype)
+
+    rest = number % 4
+
+    @pl.loop(0, (number + 1) // 4)
+    def _(i):
+        batch(4 * i, 4)
+
+    @pl.when((rest == 1) | (rest == 2))
+    def _():
+        batch(number - rest, 2)
 
 
 def finish_kernel(pieces_ref, doc_ref, out_ref):
@@ -190,7 +203,7 @@
             in_specs=[pl.BlockSpec(memory_space=pltpu.SMEM)] + vmem(len(operands)),
             out_specs=vmem(1)[0],
             scratch_shapes=[
-                pltpu.SMEM((4 * RUNS + 4,), jnp.int32),
+                pltpu.SMEM((5 * RUNS,), jnp.int32),
                 pltpu.VMEM((128, POS * 128), jnp.bfloat16),
             ],
             compiler_params=pltpu.CompilerParams(vmem_limit_bytes=32 * 2**20),

time: 106 us -> 106 us (level)
  Pallas kernels: 8.35 us -> 6.94 us
    pallas_call x2, Pallas kernels: 4.91 us -> 3.5 us  [push(): pl.pallas_call(functools.partial(push_kernel, side), out_shape=jax.ShapeD...]
  transfers between devices with their start and end apart: 3 -> 3, of which waited for: 0 -> 1; matrix products, arithmetic and copies ran while one was open for 0% -> 0% of each run, Pallas kernels for 5% -> 4%
where the time goes in v7:
time: 106 us; the launch traced here: 104 us
  blocking collectives  75.7 us (71%)
  starting transfers between devices  21 us (20%)
  Pallas kernels  6.94 us (7%)
    all_gather x1, blocking collectives, body(): own_labels = lax.all_gather(pair, 'zp', axis=0, tiled=True)  46.3 us
    all_to_all x1, blocking collectives, body(): lax.all_to_all(part.reshape(PLANE_SIZE, rows, width), PLANE, split_axis=0...  29.4 us
    ppermute x1, starting transfers between devices, body(): other_labels = lax.ppermute(own_labels, 'c', [(0, 1), (1, 0)])  9.69 us
    all_to_all x1, starting transfers between devices, body(): lax.all_to_all(spread, PLANE, split_axis=0, concat_axis=0, tiled=True)  6.9 us
    ppermute x1, starting transfers between devices, body(): neighbour = lax.ppermute(label_emb, 'zb', [(0, 1), (1, 0)])  4.37 us
    pallas_call x2, Pallas kernels, push(): pl.pallas_call(functools.partial(push_kernel, side), out_shape=jax.ShapeD...  3.5 us
    pallas_call x1, Pallas kernels, body(): pl.pallas_call(prepare_kernel, out_shape=jax.ShapeDtypeStruct((PLANE_SIZE...  2.43 us
  transfers between devices with their start and end apart: 3, of which 1 were waited for; matrix products, arithmetic and copies ran while one was open for 0% of the time, Pallas kernels for 4%

profile of v7, /device:TPU:1, one launch (start us, length us, event | category | flops | bytes accessed | tf_op | source)
XLA Modules:
  0.0 104.5 jit_solution(3756837277442987548)
XLA Ops:
  0.0 4.4 %collective-permute-start = (bf16[16,768]{1,0:T(8,128)(2,1)}, bf16[16,768]{1,0:T(8,128)(2,1)S(1)}, u32[]{:S(2)}, u32[]{:S(2)}) collective-permute-start(bf16[16,768]{1,0:T(8,128)(2,1)} %param.6), channel_id=1, source_target_pairs={{0,16},{16,0},{1,17},{17,1},{2,18},{18,2},{3,19},{19,3},{4,20},{20... | collective-permute-start | bytes 73736 | tf_op jit(solution)/shard_map/ppermute | solution.py:166
  4.4 2.4 %shard_map.55 = bf16[16,64,896]{2,1,0:T(8,128)(2,1)} custom-call(bf16[64,768]{1,0:T(8,128)(2,1)} %doc_ref.3, s32[8,1024]{1,0:T(8,128)} %bitcast.15), custom_call_target="tpu_custom_call" | custom-call | flops 393216 | bytes 8388608 | tf_op jit(solution)/shard_map/pallas_call | solution.py:167
  6.8 0.0 copy-start.2
  6.8 0.0 copy-start.3
  6.8 0.0 copy-start.1
  6.9 6.9 %all-to-all-start = ((bf16[16,64,896]{2,1,0:T(8,128)(2,1)}), bf16[16,64,896]{2,1,0:T(8,128)(2,1)S(1)}, u32[]{:S(2)}, u32[]{:S(2)}) async-start(bf16[16,64,896]{2,1,0:T(8,128)(2,1)} %shard_map.55), calls=%async_computation | async-start | bytes 3670016 | tf_op jit(solution)/shard_map/all_to_all | solution.py:180
  13.8 0.0 collective-permute-done
  13.8 0.0 copy-done.2
  13.8 0.1 multiply_reduce_fusion
  13.9 0.1 sqrt.12
  14.0 0.1 fusion
  14.1 46.3 %all_gather.3.labels_ref = bf16[512,768]{1,0:T(8,128)(2,1)S(1)} all-gather(bf16[32,768]{1,0:T(8,128)(2,1)S(1)} %fusion), channel_id=1, replica_groups=mesh['yh'=2,'zp'=16,'zb'=2,'x'=4,'yl'=2,'c'=2] {'zp'}, dimensions={0}, use_global_device_ids=true | all-gather | bytes 835584 | tf_op jit(solution)/shard_map/all_gather | solution.py:187
  60.4 9.7 %collective-permute-start.1 = (bf16[512,768]{1,0:T(8,128)(2,1)S(1)}, bf16[512,768]{1,0:T(8,128)(2,1)S(1)}, u32[]{:S(2)}, u32[]{:S(2)}) collective-permute-start(bf16[512,768]{1,0:T(8,128)(2,1)S(1)} %all_gather.3.labels_ref), channel_id=1, source_target_pairs={{0,1},{1,0},{2,3},{3,2},{4,5},{5,4},{6,7},{7,6},{8,9},{9,8},{10,11... | collective-permute-start | bytes 2359304 | tf_op jit(solution)/shard_map/ppermute | solution.py:188
  70.1 0.1 pad_add_fusion
  70.2 0.0 copy-done.3
  70.2 0.0 copy-done.1
  70.2 0.1 and_reduce_fusion
  70.4 0.0 all-to-all-done
  70.4 1.5 %shard_map.56.refs_0_ = f32[1024,768]{1,0:T(8,128)S(1)} custom-call(s32[8,256]{1,0:T(8,128)S(1)} %convert_element_type.15.live_ref, bf16[1024,896]{1,0:T(8,128)(2,1)S(1)} %bitcast.12, bf16[512,768]{1,0:T(8,128)(2,1)S(1)} %all_gather.3.labels_ref), custom_call_target="tpu_custom_call" | custom-call | flops 805306368 | bytes 6291456 | tf_op jit(solution)/shard_map/pallas_call | solution.py:200
  71.9 0.1 collective-permute-done.1.labels_ref
  72.0 2.0 %shard_map.57 = bf16[1024,768]{1,0:T(8,128)(2,1)S(1)} custom-call(s32[8,256]{1,0:T(8,128)S(1)} %convert_element_type.15.live_ref, bf16[1024,896]{1,0:T(8,128)(2,1)S(1)} %bitcast.13, bf16[512,768]{1,0:T(8,128)(2,1)S(1)} %collective-permute-done.1.labels_ref, f32[1024,768]{1,0:T(8,128)S(1)} %shard_map.56.refs_0_), custom_call_target="tpu_custom_call" | custom-call | flops 805306368 | bytes 6291456 | tf_op jit(solution)/shard_map/pallas_call | solution.py:200
  74.0 0.0 copy-start
  74.1 29.4 %all_to_all.10.pieces_ref = bf16[16,64,768]{2,1,0:T(8,128)(2,1)S(1)} all-to-all(bf16[16,64,768]{2,1,0:T(8,128)(2,1)S(1)} %bitcast.14), channel_id=1, replica_groups=mesh['yh'=2,'zp'=16,'zb'=2,'x'=4,'yl'=2,'c'=2] {'yh','x','yl'}, dimensions={0} | all-to-all | bytes 3145728 | tf_op jit(solution)/shard_map/all_to_all | solution.py:219
  103.5 0.0 copy-done
  103.5 1.0 shard_map.58
  (6 shorter events, 0.1 us)
Async XLA Ops:
  0.0 13.8 %collective-permute-start = (bf16[16,768]{1,0:T(8,128)(2,1)}, bf16[16,768]{1,0:T(8,128)(2,1)S(1)}, u32[]{:S(2)}, u32[]{:S(2)}) collective-permute-start(bf16[16,768]{1,0:T(8,128)(2,1)} %param.6), channel_id=1, source_target_pairs={{0,16},{16,0},{1,17},{17,1},{2,18},{18,2},{3,19},{19,3},{4,20},{20... | collective-permute-start | bytes 73736 | tf_op jit(solution)/shard_map/ppermute | solution.py:166
  6.8 7.0 %copy-start.2 = (bf16[16,768]{1,0:T(8,128)(2,1)S(1)}, bf16[16,768]{1,0:T(8,128)(2,1)}, u32[]{:S(2)}) copy-start(bf16[16,768]{1,0:T(8,128)(2,1)} %param.6) | copy-start | bytes 73732
  6.8 63.4 %copy-start.3 = (s32[256]{0:T(256)S(1)}, s32[256]{0:T(256)}, u32[]{:S(2)}) copy-start(s32[256]{0:T(256)} %param.8) | copy-start | bytes 3076
  6.8 63.4 %copy-start.1 = (s32[256,32]{0,1:T(8,128)S(1)}, s32[256,32]{0,1:T(8,128)}, u32[]{:S(2)}) copy-start(s32[256,32]{0,1:T(8,128)} %param.7) | copy-start | bytes 98308
  6.9 63.5 %all-to-all-start = ((bf16[16,64,896]{2,1,0:T(8,128)(2,1)}), bf16[16,64,896]{2,1,0:T(8,128)(2,1)S(1)}, u32[]{:S(2)}, u32[]{:S(2)}) async-start(bf16[16,64,896]{2,1,0:T(8,128)(2,1)} %shard_map.55), calls=%async_computation | async-start | bytes 3670016 | tf_op jit(solution)/shard_map/all_to_all | solution.py:180
  60.4 11.6 %collective-permute-start.1 = (bf16[512,768]{1,0:T(8,128)(2,1)S(1)}, bf16[512,768]{1,0:T(8,128)(2,1)S(1)}, u32[]{:S(2)}, u32[]{:S(2)}) collective-permute-start(bf16[512,768]{1,0:T(8,128)(2,1)S(1)} %all_gather.3.labels_ref), channel_id=1, source_target_pairs={{0,1},{1,0},{2,3},{3,2},{4,5},{5,4},{6,7},{7,6},{8,9},{9,8},{10,11... | collective-permute-start | bytes 2359304 | tf_op jit(solution)/shard_map/ppermute | solution.py:188
  74.0 29.4 %copy-start = (bf16[64,768]{1,0:T(8,128)(2,1)S(1)}, bf16[64,768]{1,0:T(8,128)(2,1)}, u32[]{:S(2)}) copy-start(bf16[64,768]{1,0:T(8,128)(2,1)} %doc_ref.3) | copy-start | bytes 294916

commit v8 on v7

--- a/solution.py
+++ b/solution.py
@@ -35,7 +35,7 @@
     return shard * 8 + yh * 4, (shard + 1 - 2 * core) * 8 + yh * 4
 
 
-def prepare_kernel(doc_ref, pos_ref, spread_ref, packed, sems):
+def prepare_kernel(doc_ref, pos_ref, blocks_ref, len_ref, spread_ref, live_ref, packed, sems):
     rows, width = doc_ref.shape
     packed[:, :width] = unit_rows(doc_ref[...])[0].astype(jnp.bfloat16)
     _, _, _, x, yl, core = place()
@@ -55,6 +55,13 @@
     ]
     for copy in copies:
         copy.start()
+    listed = blocks_ref[...]
+    slot = lax.broadcasted_iota(jnp.int32, listed.shape, 0)
+    listed = jnp.where(slot < len_ref[...], listed, -1)
+    for i in range(8):
+        block = first_blocks()[i // 4] + i % 4
+        hits = jnp.where(listed == block, 1, 0)
+        live_ref[i : i + 1, :] = jnp.max(hits, axis=0, keepdims=True)
     for copy in copies:
         copy.wait()
 
@@ -164,11 +171,14 @@
 def body(doc_emb, label_emb, short_blocks, short_len, positives):
     rows, width = doc_emb.shape
     neighbour = lax.ppermute(label_emb, "zb", [(0, 1), (1, 0)])
-    spread = pl.pallas_call(
+    spread, live = pl.pallas_call(
         prepare_kernel,
-        out_shape=jax.ShapeDtypeStruct((PLANE_SIZE, rows, width + 128), jnp.bfloat16),
-        in_specs=vmem(2),
-        out_specs=pl.BlockSpec(memory_space=pl.ANY),
+        out_shape=(
+            jax.ShapeDtypeStruct((PLANE_SIZE, rows, width + 128), jnp.bfloat16),
+            jax.ShapeDtypeStruct((8, short_blocks.shape[0]), jnp.int32),
+        ),
+        in_specs=vmem(4),
+        out_specs=(pl.BlockSpec(memory_space=pl.ANY), vmem(1)[0]),
         scratch_shapes=[
             pltpu.VMEM((rows, width + 128), jnp.bfloat16),
             pltpu.SemaphoreType.DMA((PLANE_SIZE,)),
@@ -176,7 +186,7 @@
         cost_estimate=pl.CostEstimate(
             flops=8 * rows * width, bytes_accessed=8 * 2**20, transcendentals=rows
         ),
-    )(doc_emb, positives.T)
+    )(doc_emb, positives.T, short_blocks.T, short_len.reshape(1, -1))
     docs = lax.all_to_all(spread, PLANE, split_axis=0, concat_axis=0, tiled=True)
     docs = docs.reshape(PLANE_SIZE * rows, width + 128)
     even = lax.axis_index("zb") == 0
@@ -186,15 +196,6 @@
     pair = unit_rows(pair)[0].astype(jnp.bfloat16)
     own_labels = lax.all_gather(pair, "zp", axis=0, tiled=True)
     other_labels = lax.ppermute(own_labels, "c", [(0, 1), (1, 0)])
-
-    grid = jnp.arange(4, dtype=jnp.int32)
-    block_ids = jnp.concatenate([first + grid for first in first_blocks()])
-    slot = jnp.arange(short_blocks.shape[1], dtype=jnp.int32)
-    live = jnp.any(
-        (short_blocks.T[None] == block_ids[:, None, None])
-        & (slot[:, None] < short_len[None, :])[None],
-        axis=1,
-    ).astype(jnp.int32)
 
     def push(side, dtype, *operands):
         return pl.pallas_call(

time: 106 us -> 106 us (level)
  no operation moved by 1% of the time
where the time goes in v8:
time: 106 us; the launch traced here: 104 us
  blocking collectives  75.1 us (71%)
  starting transfers between devices  20.8 us (20%)
  Pallas kernels  7.22 us (7%)
    all_gather x1, blocking collectives, body(): own_labels = lax.all_gather(pair, 'zp', axis=0, tiled=True)  46.3 us
    all_to_all x1, blocking collectives, body(): lax.all_to_all(part.reshape(PLANE_SIZE, rows, width), PLANE, split_axis=0...  28.8 us
    ppermute x1, starting transfers between devices, body(): other_labels = lax.ppermute(own_labels, 'c', [(0, 1), (1, 0)])  9.7 us
    all_to_all x1, starting transfers between devices, body(): lax.all_to_all(spread, PLANE, split_axis=0, concat_axis=0, tiled=True)  6.77 us
    ppermute x1, starting transfers between devices, body(): neighbour = lax.ppermute(label_emb, 'zb', [(0, 1), (1, 0)])  4.37 us
    pallas_call x2, Pallas kernels, push(): pl.pallas_call(functools.partial(push_kernel, side), out_shape=jax.ShapeD...  3.13 us
    pallas_call x1, Pallas kernels, body(): pl.pallas_call(prepare_kernel, out_shape=(jax.ShapeDtypeStruct((PLANE_SIZ...  3.08 us
  transfers between devices with their start and end apart: 3, of which 1 were waited for; matrix products, arithmetic and copies ran while one was open for 0% of the time, Pallas kernels for 4%

profile of v8, /device:TPU:1, one launch (start us, length us, event | category | flops | bytes accessed | tf_op | source)
XLA Modules:
  0.0 104.0 jit_solution(5169534825537763203)
XLA Ops:
  0.0 4.4 %collective-permute-start = (bf16[16,768]{1,0:T(8,128)(2,1)}, bf16[16,768]{1,0:T(8,128)(2,1)S(1)}, u32[]{:S(2)}, u32[]{:S(2)}) collective-permute-start(bf16[16,768]{1,0:T(8,128)(2,1)} %param.6), channel_id=1, source_target_pairs={{0,16},{16,0},{1,17},{17,1},{2,18},{18,2},{3,19},{19,3},{4,20},{20... | collective-permute-start | bytes 73736 | tf_op jit(solution)/shard_map/ppermute | solution.py:173
  4.4 3.1 %shard_map.55 = (bf16[16,64,896]{2,1,0:T(8,128)(2,1)}, s32[8,256]{1,0:T(8,128)}) custom-call(bf16[64,768]{1,0:T(8,128)(2,1)} %doc_ref.3, s32[8,1024]{1,0:T(8,128)} %bitcast.16, s32[32,256]{1,0:T(8,128)} %bitcast.17, s32[1,256]{1,0:T(1,128)} %bitcast.18), custom_call_target="tpu_custom_call" | custom-call | flops 393216 | bytes 8388608 | tf_op jit(solution)/shard_map/pallas_call | solution.py:174
  7.5 0.0 copy-start.2
  7.5 0.0 copy-start.1
  7.5 6.8 %all-to-all-start = ((bf16[16,64,896]{2,1,0:T(8,128)(2,1)}), bf16[16,64,896]{2,1,0:T(8,128)(2,1)S(1)}, u32[]{:S(2)}, u32[]{:S(2)}) async-start(bf16[16,64,896]{2,1,0:T(8,128)(2,1)} %get-tuple-element.8), calls=%async_computation | async-start | bytes 3670016 | tf_op jit(solution)/shard_map/all_to_all | solution.py:190
  14.3 0.0 collective-permute-done
  14.3 0.0 copy-done.2
  14.3 0.1 multiply_reduce_fusion
  14.4 0.1 sqrt.12
  14.5 0.1 fusion
  14.6 46.3 %all_gather.3.labels_ref = bf16[512,768]{1,0:T(8,128)(2,1)S(1)} all-gather(bf16[32,768]{1,0:T(8,128)(2,1)S(1)} %fusion), channel_id=1, replica_groups=mesh['yh'=2,'zp'=16,'zb'=2,'x'=4,'yl'=2,'c'=2] {'zp'}, dimensions={0}, use_global_device_ids=true | all-gather | bytes 835584 | tf_op jit(solution)/shard_map/all_gather | solution.py:197
  60.9 9.7 %collective-permute-start.1 = (bf16[512,768]{1,0:T(8,128)(2,1)S(1)}, bf16[512,768]{1,0:T(8,128)(2,1)S(1)}, u32[]{:S(2)}, u32[]{:S(2)}) collective-permute-start(bf16[512,768]{1,0:T(8,128)(2,1)S(1)} %all_gather.3.labels_ref), channel_id=1, source_target_pairs={{0,1},{1,0},{2,3},{3,2},{4,5},{5,4},{6,7},{7,6},{8,9},{9,8},{10,11... | collective-permute-start | bytes 2359304 | tf_op jit(solution)/shard_map/ppermute | solution.py:198
  70.6 0.0 all-to-all-done
  70.6 0.0 copy-done.1
  70.6 1.5 %shard_map.56.refs_0_ = f32[1024,768]{1,0:T(8,128)S(1)} custom-call(s32[8,256]{1,0:T(8,128)S(1)} %copy-done.1, bf16[1024,896]{1,0:T(8,128)(2,1)S(1)} %bitcast.13, bf16[512,768]{1,0:T(8,128)(2,1)S(1)} %all_gather.3.labels_ref), custom_call_target="tpu_custom_call" | custom-call | flops 805306368 | bytes 6291456 | tf_op jit(solution)/shard_map/pallas_call | solution.py:201
  72.1 0.4 collective-permute-done.1.labels_ref
  72.5 1.7 %shard_map.57 = bf16[1024,768]{1,0:T(8,128)(2,1)S(1)} custom-call(s32[8,256]{1,0:T(8,128)S(1)} %copy-done.1, bf16[1024,896]{1,0:T(8,128)(2,1)S(1)} %bitcast.14, bf16[512,768]{1,0:T(8,128)(2,1)S(1)} %collective-permute-done.1.labels_ref, f32[1024,768]{1,0:T(8,128)S(1)} %shard_map.56.refs_0_), custom_call_target="tpu_custom_call" | custom-call | flops 805306368 | bytes 6291456 | tf_op jit(solution)/shard_map/pallas_call | solution.py:201
  74.2 0.0 copy-start
  74.2 28.8 %all_to_all.10.pieces_ref = bf16[16,64,768]{2,1,0:T(8,128)(2,1)S(1)} all-to-all(bf16[16,64,768]{2,1,0:T(8,128)(2,1)S(1)} %bitcast.15), channel_id=1, replica_groups=mesh['yh'=2,'zp'=16,'zb'=2,'x'=4,'yl'=2,'c'=2] {'yh','x','yl'}, dimensions={0} | all-to-all | bytes 3145728 | tf_op jit(solution)/shard_map/all_to_all | solution.py:220
  103.0 0.0 copy-done
  103.0 1.0 shard_map.58
  (3 shorter events, 0.0 us)
Async XLA Ops:
  0.0 14.3 %collective-permute-start = (bf16[16,768]{1,0:T(8,128)(2,1)}, bf16[16,768]{1,0:T(8,128)(2,1)S(1)}, u32[]{:S(2)}, u32[]{:S(2)}) collective-permute-start(bf16[16,768]{1,0:T(8,128)(2,1)} %param.6), channel_id=1, source_target_pairs={{0,16},{16,0},{1,17},{17,1},{2,18},{18,2},{3,19},{19,3},{4,20},{20... | collective-permute-start | bytes 73736 | tf_op jit(solution)/shard_map/ppermute | solution.py:173
  7.5 6.8 %copy-start.2 = (bf16[16,768]{1,0:T(8,128)(2,1)S(1)}, bf16[16,768]{1,0:T(8,128)(2,1)}, u32[]{:S(2)}) copy-start(bf16[16,768]{1,0:T(8,128)(2,1)} %param.6) | copy-start | bytes 73732
  7.5 63.2 %copy-start.1 = (s32[8,256]{1,0:T(8,128)S(1)}, s32[8,256]{1,0:T(8,128)}, u32[]{:S(2)}) copy-start(s32[8,256]{1,0:T(8,128)} %get-tuple-element.7.live_ref) | copy-start | bytes 24580
  7.5 63.1 %all-to-all-start = ((bf16[16,64,896]{2,1,0:T(8,128)(2,1)}), bf16[16,64,896]{2,1,0:T(8,128)(2,1)S(1)}, u32[]{:S(2)}, u32[]{:S(2)}) async-start(bf16[16,64,896]{2,1,0:T(8,128)(2,1)} %get-tuple-element.8), calls=%async_computation | async-start | bytes 3670016 | tf_op jit(solution)/shard_map/all_to_all | solution.py:190
  60.9 11.6 %collective-permute-start.1 = (bf16[512,768]{1,0:T(8,128)(2,1)S(1)}, bf16[512,768]{1,0:T(8,128)(2,1)S(1)}, u32[]{:S(2)}, u32[]{:S(2)}) collective-permute-start(bf16[512,768]{1,0:T(8,128)(2,1)S(1)} %all_gather.3.labels_ref), channel_id=1, source_target_pairs={{0,1},{1,0},{2,3},{3,2},{4,5},{5,4},{6,7},{7,6},{8,9},{9,8},{10,11... | collective-permute-start | bytes 2359304 | tf_op jit(solution)/shard_map/ppermute | solution.py:198
  74.2 28.8 %copy-start = (bf16[64,768]{1,0:T(8,128)(2,1)S(1)}, bf16[64,768]{1,0:T(8,128)(2,1)}, u32[]{:S(2)}) copy-start(bf16[64,768]{1,0:T(8,128)(2,1)} %doc_ref.3) | copy-start | bytes 294916

commit v9 on v7

--- a/solution.py
+++ b/solution.py
@@ -64,7 +64,7 @@
     _, zp, zb, _, _, _ = place()
     width = labels_ref.shape[1]
     first = first_blocks()[side]
-    lane = lax.broadcasted_iota(jnp.int32, (1, LAB_BLK), 1)
+    lane = lax.broadcasted_iota(jnp.int32, (1, LAB_BLK), 1) ^ (16 * zb)
 
     row = lax.broadcasted_iota(jnp.int32, select.shape, 0)
     group = lax.broadcasted_iota(jnp.int32, select.shape, 1) // 128
@@ -179,10 +179,7 @@
     )(doc_emb, positives.T)
     docs = lax.all_to_all(spread, PLANE, split_axis=0, concat_axis=0, tiled=True)
     docs = docs.reshape(PLANE_SIZE * rows, width + 128)
-    even = lax.axis_index("zb") == 0
-    pair = jnp.stack(
-        [jnp.where(even, label_emb, neighbour), jnp.where(even, neighbour, label_emb)]
-    ).reshape(2 * label_emb.shape[0], width)
+    pair = jnp.concatenate([label_emb, neighbour], axis=0)
     pair = unit_rows(pair)[0].astype(jnp.bfloat16)
     own_labels = lax.all_gather(pair, "zp", axis=0, tiled=True)
     other_labels = lax.ppermute(own_labels, "c", [(0, 1), (1, 0)])

time: 106 us -> 112 us (1.057)
  blocking collectives: 75.7 us -> 78.3 us
  Pallas kernels: 6.94 us -> 8.67 us
  starting transfers between devices: 21 us -> 22.6 us
    all_gather x1, blocking collectives: 46.3 us -> 48.6 us  [body(): own_labels = lax.all_gather(pair, 'zp', axis=0, tiled=True)]
    pallas_call x2, Pallas kernels: 3.5 us -> 5.22 us  [push(): pl.pallas_call(functools.partial(push_kernel, side), out_shape=jax.ShapeD...]
    ppermute x1, starting transfers between devices: 9.69 us -> 11.3 us  [body(): other_labels = lax.ppermute(own_labels, 'c', [(0, 1), (1, 0)])]
    ppermute x1, waiting for transfers between devices: 0.01 us -> 1.2 us  [body(): neighbour = lax.ppermute(label_emb, 'zb', [(0, 1), (1, 0)])]
  transfers between devices with their start and end apart: 3 -> 3, of which waited for: 1 -> 1; matrix products, arithmetic and copies ran while one was open for 0% -> 0% of each run, Pallas kernels for 4% -> 2%
where the time goes in v9:
time: 112 us; the launch traced here: 111 us
  blocking collectives  78.3 us (70%)
  starting transfers between devices  22.6 us (20%)
  Pallas kernels  8.67 us (8%)
  waiting for transfers between devices  1.21 us (1%)
    all_gather x1, blocking collectives, body(): own_labels = lax.all_gather(pair, 'zp', axis=0, tiled=True)  48.6 us
    all_to_all x1, blocking collectives, body(): lax.all_to_all(part.reshape(PLANE_SIZE, rows, width), PLANE, split_axis=0...  29.7 us
    ppermute x1, starting transfers between devices, body(): other_labels = lax.ppermute(own_labels, 'c', [(0, 1), (1, 0)])  11.3 us
    all_to_all x1, starting transfers between devices, body(): lax.all_to_all(spread, PLANE, split_axis=0, concat_axis=0, tiled=True)  7.73 us
    pallas_call x2, Pallas kernels, push(): pl.pallas_call(functools.partial(push_kernel, side), out_shape=jax.ShapeD...  5.22 us
    ppermute x1, starting transfers between devices, body(): neighbour = lax.ppermute(label_emb, 'zb', [(0, 1), (1, 0)])  3.55 us
    pallas_call x1, Pallas kernels, body(): pl.pallas_call(prepare_kernel, out_shape=jax.ShapeDtypeStruct((PLANE_SIZE...  2.43 us
  transfers between devices with their start and end apart: 3, of which 1 were waited for; matrix products, arithmetic and copies ran while one was open for 0% of the time, Pallas kernels for 2%

profile of v9, /device:TPU:1, one launch (start us, length us, event | category | flops | bytes accessed | tf_op | source)
XLA Modules:
  0.0 111.4 jit_solution(17372974052251096152)
XLA Ops:
  0.0 2.4 %shard_map.55 = bf16[16,64,896]{2,1,0:T(8,128)(2,1)} custom-call(bf16[64,768]{1,0:T(8,128)(2,1)} %doc_ref.3, s32[8,1024]{1,0:T(8,128)} %bitcast.7), custom_call_target="tpu_custom_call" | custom-call | flops 393216 | bytes 8388608 | tf_op jit(solution)/shard_map/pallas_call | solution.py:167
  2.4 0.0 copy-start.1
  2.5 0.0 copy-start.3
  2.5 0.0 copy-start.2
  2.5 7.7 %all-to-all-start = ((bf16[16,64,896]{2,1,0:T(8,128)(2,1)}), bf16[16,64,896]{2,1,0:T(8,128)(2,1)S(1)}, u32[]{:S(2)}, u32[]{:S(2)}) async-start(bf16[16,64,896]{2,1,0:T(8,128)(2,1)} %shard_map.55), calls=%async_computation | async-start | bytes 3670016 | tf_op jit(solution)/shard_map/all_to_all | solution.py:180
  10.2 0.0 copy-done.1
  10.2 3.5 %collective-permute-start = (bf16[16,768]{1,0:T(8,128)(2,1)S(1)}, bf16[16,768]{1,0:T(8,128)(2,1)S(1)}, u32[]{:S(2)}, u32[]{:S(2)}) collective-permute-start(bf16[16,768]{1,0:T(8,128)(2,1)S(1)} %copy-done.1), channel_id=1, source_target_pairs={{0,16},{16,0},{1,17},{17,1},{2,18},{18,2},{3,19},{19,3},{4,20},{20... | collective-permute-start | bytes 73736 | tf_op jit(solution)/shard_map/ppermute | solution.py:166
  13.8 1.2 %collective-permute-done = bf16[16,768]{1,0:T(8,128)(2,1)S(1)} collective-permute-done((bf16[16,768]{1,0:T(8,128)(2,1)S(1)}, bf16[16,768]{1,0:T(8,128)(2,1)S(1)}, u32[]{:S(2)}, u32[]{:S(2)}) %collective-permute-start) | collective-permute-done | bytes 24608 | tf_op jit(solution)/shard_map/ppermute | solution.py:166
  15.0 0.1 fusion
  15.1 0.1 fusion.1
  15.2 48.6 %all_gather.3.labels_ref = bf16[512,768]{1,0:T(8,128)(2,1)S(1)} all-gather(bf16[32,768]{1,0:T(8,128)(2,1)S(1)} %fusion.1), channel_id=1, replica_groups=mesh['yh'=2,'zp'=16,'zb'=2,'x'=4,'yl'=2,'c'=2] {'zp'}, dimensions={0}, use_global_device_ids=true | all-gather | bytes 835584 | tf_op jit(solution)/shard_map/all_gather | solution.py:184
  63.8 11.3 %collective-permute-start.1 = (bf16[512,768]{1,0:T(8,128)(2,1)S(1)}, bf16[512,768]{1,0:T(8,128)(2,1)S(1)}, u32[]{:S(2)}, u32[]{:S(2)}) collective-permute-start(bf16[512,768]{1,0:T(8,128)(2,1)S(1)} %all_gather.3.labels_ref), channel_id=1, source_target_pairs={{0,1},{1,0},{2,3},{3,2},{4,5},{5,4},{6,7},{7,6},{8,9},{9,8},{10,11... | collective-permute-start | bytes 2359304 | tf_op jit(solution)/shard_map/ppermute | solution.py:185
  75.1 0.1 pad_add_fusion
  75.2 0.0 copy-done.3
  75.2 0.0 copy-done.2
  75.2 0.1 and_reduce_fusion
  75.4 0.0 all-to-all-done
  75.4 2.5 %shard_map.56.refs_0_ = f32[1024,768]{1,0:T(8,128)S(1)} custom-call(s32[8,256]{1,0:T(8,128)S(1)} %convert_element_type.9.live_ref, bf16[1024,896]{1,0:T(8,128)(2,1)S(1)} %bitcast.4, bf16[512,768]{1,0:T(8,128)(2,1)S(1)} %all_gather.3.labels_ref), custom_call_target="tpu_custom_call" | custom-call | flops 805306368 | bytes 6291456 | tf_op jit(solution)/shard_map/pallas_call | solution.py:197
  77.9 0.0 collective-permute-done.1.labels_ref
  77.9 2.7 %shard_map.57 = bf16[1024,768]{1,0:T(8,128)(2,1)S(1)} custom-call(s32[8,256]{1,0:T(8,128)S(1)} %convert_element_type.9.live_ref, bf16[1024,896]{1,0:T(8,128)(2,1)S(1)} %bitcast.5, bf16[512,768]{1,0:T(8,128)(2,1)S(1)} %collective-permute-done.1.labels_ref, f32[1024,768]{1,0:T(8,128)S(1)} %shard_map.56.refs_0_), custom_call_target="tpu_custom_call" | custom-call | flops 805306368 | bytes 6291456 | tf_op jit(solution)/shard_map/pallas_call | solution.py:197
  80.6 0.0 copy-start
  80.6 29.7 %all_to_all.10.pieces_ref = bf16[16,64,768]{2,1,0:T(8,128)(2,1)S(1)} all-to-all(bf16[16,64,768]{2,1,0:T(8,128)(2,1)S(1)} %bitcast.6), channel_id=1, replica_groups=mesh['yh'=2,'zp'=16,'zb'=2,'x'=4,'yl'=2,'c'=2] {'yh','x','yl'}, dimensions={0} | all-to-all | bytes 3145728 | tf_op jit(solution)/shard_map/all_to_all | solution.py:216
  110.3 0.0 copy-done
  110.3 1.0 shard_map.58
  (4 shorter events, 0.0 us)
Async XLA Ops:
  2.4 7.8 %copy-start.1 = (bf16[16,768]{1,0:T(8,128)(2,1)S(1)}, bf16[16,768]{1,0:T(8,128)(2,1)}, u32[]{:S(2)}) copy-start(bf16[16,768]{1,0:T(8,128)(2,1)} %param.6) | copy-start | bytes 73732
  2.5 72.7 %copy-start.3 = (s32[256]{0:T(256)S(1)}, s32[256]{0:T(256)}, u32[]{:S(2)}) copy-start(s32[256]{0:T(256)} %param.8) | copy-start | bytes 3076
  2.5 72.7 %copy-start.2 = (s32[256,32]{0,1:T(8,128)S(1)}, s32[256,32]{0,1:T(8,128)}, u32[]{:S(2)}) copy-start(s32[256,32]{0,1:T(8,128)} %param.7) | copy-start | bytes 98308
  2.5 72.9 %all-to-all-start = ((bf16[16,64,896]{2,1,0:T(8,128)(2,1)}), bf16[16,64,896]{2,1,0:T(8,128)(2,1)S(1)}, u32[]{:S(2)}, u32[]{:S(2)}) async-start(bf16[16,64,896]{2,1,0:T(8,128)(2,1)} %shard_map.55), calls=%async_computation | async-start | bytes 3670016 | tf_op jit(solution)/shard_map/all_to_all | solution.py:180
  10.2 4.8 %collective-permute-start = (bf16[16,768]{1,0:T(8,128)(2,1)S(1)}, bf16[16,768]{1,0:T(8,128)(2,1)S(1)}, u32[]{:S(2)}, u32[]{:S(2)}) collective-permute-start(bf16[16,768]{1,0:T(8,128)(2,1)S(1)} %copy-done.1), channel_id=1, source_target_pairs={{0,16},{16,0},{1,17},{17,1},{2,18},{18,2},{3,19},{19,3},{4,20},{20... | collective-permute-start | bytes 73736 | tf_op jit(solution)/shard_map/ppermute | solution.py:166
  63.8 14.1 %collective-permute-start.1 = (bf16[512,768]{1,0:T(8,128)(2,1)S(1)}, bf16[512,768]{1,0:T(8,128)(2,1)S(1)}, u32[]{:S(2)}, u32[]{:S(2)}) collective-permute-start(bf16[512,768]{1,0:T(8,128)(2,1)S(1)} %all_gather.3.labels_ref), channel_id=1, source_target_pairs={{0,1},{1,0},{2,3},{3,2},{4,5},{5,4},{6,7},{7,6},{8,9},{9,8},{10,11... | collective-permute-start | bytes 2359304 | tf_op jit(solution)/shard_map/ppermute | solution.py:185
  80.6 29.7 %copy-start = (bf16[64,768]{1,0:T(8,128)(2,1)S(1)}, bf16[64,768]{1,0:T(8,128)(2,1)}, u32[]{:S(2)}) copy-start(bf16[64,768]{1,0:T(8,128)(2,1)} %doc_ref.3) | copy-start | bytes 294916
